TPU v7x, 32 devices: a whole 2x2x4 slice. The times are simulated.
32 devices in a mesh: rep: 4 (over z), tp: 8 (over y, x, core).
Axes of the slice: x: 2, y: 2, z: 4, core: 2. Of those that a mesh axis runs over, the one named last changes fastest.
Arguments:
- queries: bfloat16 [64, 5, 8192], P('rep', None, 'tp'), may hold values from -120 to 120
- kv_cache: bfloat16 [64, 2, 256, 512], P('rep'), may hold values from -6 to 6
- kv_new: bfloat16 [64, 2, 5, 512], P('rep'), may hold values from -6 to 6
- cache_len: int32 [64], P('rep'), may hold values from 2 to 256, as said below
- out_proj: bfloat16 [8192, 16384], P('tp'), may hold values from -0.09375 to 0.09375
- residual: bfloat16 [64, 5, 16384], P('rep', None, 'tp'), may hold values from -6 to 6
- accepted: int32 [64], P('rep'), may hold values from 0 to 4
- draft_emb: bfloat16 [64, 5, 16384], P('tp'), may hold values from -6 to 6
- draft_gain: bfloat16 [16384], replicated, may hold values from 0.25 to 1.75
- draft_proj: bfloat16 [16384, 16384], P('tp', 'rep'), may hold values from -0.0625 to 0.0625
Outputs:
- verified: bfloat16 [64, 5, 16384], P('rep', None, 'tp')
- draft_features: bfloat16 [64, 16384], P('tp')
Inputs may be any that keep to these rules, and one draw needn't show every extreme that they name: `cache_len`: some row has exactly 2 filled slots and some row all 256.
All inputs are finite; a program needn't handle non-finite values.
Results may differ from a plain program's by a relative error of at most 0.0055.
Values may be sent and summed in bfloat16 or wider, within the bound.
A program may use at most 128 MiB of HBM per device.

v0:
```python
import jax
import jax.numpy as jnp
from jax import lax
from jax.sharding import PartitionSpec as P

HEADS = 64
KV_HEADS = 4
HEAD_DIM = 128
DRAFT = 5
CACHE = 256


def attend(queries, cache_keys, cache_vals, fresh_keys, fresh_vals, cache_len):
    row_count, draft_len, width = queries.shape
    group = width // HEAD_DIM
    scale = HEAD_DIM ** (-0.5)
    query_all = queries.reshape(row_count, draft_len, group, HEAD_DIM)
    cache_scores = (
        jnp.einsum("rjgd,rpd->rjgp", query_all, cache_keys, preferred_element_type=jnp.float32)
        * scale
    )
    positions = jnp.arange(CACHE, dtype=jnp.int32)
    valid = positions[None, :] < cache_len[:, None]
    cache_scores = jnp.where(valid[:, None, None, :], cache_scores, -jnp.inf)
    fresh_scores = (
        jnp.einsum("rjgd,rid->rjgi", query_all, fresh_keys, preferred_element_type=jnp.float32)
        * scale
    )
    causal = jnp.arange(draft_len)[None, :] <= jnp.arange(draft_len)[:, None]
    fresh_scores = jnp.where(causal[None, :, None, :], fresh_scores, -jnp.inf)
    highest = jnp.maximum(jnp.max(cache_scores, -1), jnp.max(fresh_scores, -1))[..., None]
    cache_exp = jnp.exp(cache_scores - highest)
    fresh_exp = jnp.exp(fresh_scores - highest)
    total = jnp.sum(cache_exp, -1, keepdims=True) + jnp.sum(fresh_exp, -1, keepdims=True)
    cache_weights = (cache_exp / total).astype(jnp.bfloat16)
    fresh_weights = (fresh_exp / total).astype(jnp.bfloat16)
    mixed = jnp.einsum(
        "rjgp,rpd->rjgd", cache_weights, cache_vals, preferred_element_type=jnp.float32
    )
    mixed = mixed + jnp.einsum(
        "rjgi,rid->rjgd", fresh_weights, fresh_vals, preferred_element_type=jnp.float32
    )
    return mixed.reshape(row_count, draft_len, width).astype(jnp.bfloat16)


def local(
    queries,
    kv_cache,
    kv_new,
    cache_len,
    out_proj,
    residual,
    accepted,
    draft_emb,
    draft_gain,
    draft_proj,
):
    row_count, draft_len, width = queries.shape
    local_heads = width // HEAD_DIM
    group = HEADS // KV_HEADS
    kv_start = lax.axis_index("tp") * local_heads // group * HEAD_DIM
    own_cache = lax.dynamic_slice_in_dim(kv_cache, kv_start, HEAD_DIM, 3)
    own_fresh = lax.dynamic_slice_in_dim(kv_new, kv_start, HEAD_DIM, 3)
    attn = attend(
        queries, own_cache[:, 0], own_cache[:, 1], own_fresh[:, 0], own_fresh[:, 1], cache_len
    )
    projected = jnp.dot(
        attn.reshape(row_count * draft_len, width), out_proj, preferred_element_type=jnp.float32
    )
    feature_width = residual.shape[2]
    summed = lax.psum(projected, "tp")
    own_sums = lax.dynamic_slice_in_dim(
        summed, lax.axis_index("tp") * feature_width, feature_width, 1
    )
    verified = (
        residual.astype(jnp.float32) + own_sums.reshape(row_count, draft_len, feature_width)
    ).astype(jnp.bfloat16)
    picked = jnp.arange(draft_len, dtype=jnp.int32)[None, :] == accepted[:, None]
    feature = jnp.sum(
        jnp.where(picked[:, :, None], verified.astype(jnp.float32), 0.0), axis=1
    ).astype(jnp.bfloat16)
    every_row = lax.all_gather(feature, "rep", axis=0, tiled=True)
    owned = lax.all_to_all(every_row, "tp", split_axis=0, concat_axis=1, tiled=True)
    state = owned.astype(jnp.float32)
    gain_values = draft_gain.astype(jnp.float32)
    for draft_step in range(DRAFT):
        mixed = state + draft_emb[:, draft_step].astype(jnp.float32)
        inverse = lax.rsqrt(jnp.mean(mixed * mixed, axis=1, keepdims=True) + 1e-05)
        normed = (mixed * inverse * gain_values).astype(jnp.bfloat16)
        input_cols = lax.all_to_all(normed, "tp", split_axis=1, concat_axis=0, tiled=True)
        own_update = lax.psum_scatter(
            jnp.dot(input_cols, draft_proj, preferred_element_type=jnp.float32),
            "tp",
            scatter_dimension=0,
            tiled=True,
        )
        update = lax.all_gather(own_update, "rep", axis=1, tiled=True)
        state = state + jax.nn.silu(update)
    return (verified, state.astype(jnp.bfloat16))


def solution(mesh):
    in_specs = (
        P("rep", None, "tp"),
        P("rep", None, None, None),
        P("rep", None, None, None),
        P("rep"),
        P("tp", None),
        P("rep", None, "tp"),
        P("rep"),
        P("tp", None, None),
        P(),
        P("tp", "rep"),
    )
    out_specs = (P("rep", None, "tp"), P("tp", None))
    return jax.shard_map(local, mesh=mesh, in_specs=in_specs, out_specs=out_specs, check_vma=False)
```

profile of v0, /device:TPU:0, one launch (start us, length us, event | category | flops | bytes accessed | tf_op | source)
XLA Modules:
  0.0 518.4 jit_solution(17805425932413170924)
XLA Ops:
  14.9 16.0 %fusion.20 = f32[80,16384]{1,0:T(8,128)} fusion(bf16[1024,16384]{1,0:T(8,128)(2,1)} %param.14, bf16[10,8,8,128]{3,2,1,0:T(8,128)(2,1)S(1)} %bitcast.120), kind=kOutput, calls=%fused_computation.51 | convolution fusion | flops 2684354560 | bytes 38961152 | tf_op jit(solution)/shard_map/dot_general | solution.py:67
  31.1 95.4 %all-reduce.2.cloned.1.call-done = f32[80,16384]{1,0:T(8,128)} async-done(((f32[80,16384]{1,0:T(8,128)}), f32[80,16384]{1,0:T(8,128)}) %all-reduce.2.cloned.1.call-update) | async-done | bytes 5242896 | tf_op jit(solution)/shard_map/psum | solution.py:71
  128.3 14.6 %all_gather.18 = bf16[64,2048]{1,0:T(8,128)(2,1)} all-gather(bf16[16,2048]{1,0:T(8,128)(2,1)S(1)} %get-tuple-element.12), channel_id=1, replica_groups=mesh['rep'=4,'tp'=8] {'rep'}, dimensions={0}, use_global_device_ids=true | all-gather | bytes 327680 | tf_op jit(solution)/shard_map/all_gather | solution.py:82
  146.4 6.7 %all-to-all-done = bf16[8,8,2048]{2,1,0:T(8,128)(2,1)S(1)} async-done(((bf16[8,8,2048]{2,1,0:T(8,128)(2,1)}), bf16[8,8,2048]{2,1,0:T(8,128)(2,1)S(1)}, u32[]{:S(2)}, u32[]{:S(2)}) %all-to-all-start) | async-done | bytes 262176 | tf_op jit(solution)/shard_map/all_to_all | solution.py:83
  153.5 9.3 %all_to_all.105 = bf16[8,8,2048]{2,0,1:T(8,128)(2,1)S(1)} all-to-all(bf16[8,8,2048]{2,0,1:T(8,128)(2,1)S(1)} %multiply_convert_fusion.4), channel_id=1, replica_groups=mesh['rep'=4,'tp'=8] {'tp'}, dimensions={1} | all-to-all | bytes 524288 | tf_op jit(solution)/shard_map/all_to_all | solution.py:90
  162.9 9.8 %fusion.18 = f32[64,4096]{1,0:T(8,128)} fusion(bf16[2048,4096]{1,0:T(8,128)(2,1)} %param.19, bf16[8,8,2048]{2,0,1:T(8,128)(2,1)S(1)} %all_to_all.105), kind=kOutput, calls=%fused_computation.49 | convolution fusion | flops 1073741824 | bytes 18087936 | tf_op jit(solution)/shard_map/dot_general | solution.py:92
  172.8 35.7 %reduce-scatter.6.cloned.1.call-done = f32[8,4096]{1,0:T(8,128)} async-done(((f32[64,4096]{1,0:T(8,128)}), f32[8,4096]{1,0:T(8,128)}) %reduce-scatter.6.cloned.1.call-update) | async-done | bytes 131088 | tf_op jit(solution)/shard_map/reduce_scatter | solution.py:91
  208.5 15.8 %all_gather.19 = f32[8,16384]{1,0:T(8,128)S(1)} all-gather(f32[8,4096]{1,0:T(8,128)} %reduce-scatter.6.cloned.1.call-done), channel_id=1, replica_groups=mesh['rep'=4,'tp'=8] {'rep'}, dimensions={1}, use_global_device_ids=true | all-gather | bytes 655360 | tf_op jit(solution)/shard_map/all_gather | solution.py:97
  224.7 9.5 %all_to_all.106 = bf16[8,8,2048]{2,0,1:T(8,128)(2,1)S(1)} all-to-all(bf16[8,8,2048]{2,0,1:T(8,128)(2,1)S(1)} %bitcast.117), channel_id=1, replica_groups=mesh['rep'=4,'tp'=8] {'tp'}, dimensions={1} | all-to-all | bytes 524288 | tf_op jit(solution)/shard_map/all_to_all | solution.py:90
  234.2 9.8 %fusion.16 = f32[64,4096]{1,0:T(8,128)} fusion(bf16[2048,4096]{1,0:T(8,128)(2,1)} %param.19, bf16[8,8,2048]{2,0,1:T(8,128)(2,1)S(1)} %all_to_all.106), kind=kOutput, calls=%fused_computation.47 | convolution fusion | flops 1073741824 | bytes 18087936 | tf_op jit(solution)/shard_map/dot_general | solution.py:92
  244.1 36.0 %reduce-scatter.8.cloned.1.call-done = f32[8,4096]{1,0:T(8,128)} async-done(((f32[64,4096]{1,0:T(8,128)}), f32[8,4096]{1,0:T(8,128)}) %reduce-scatter.8.cloned.1.call-update) | async-done | bytes 131088 | tf_op jit(solution)/shard_map/reduce_scatter | solution.py:91
  280.1 16.0 %all_gather.20 = f32[8,16384]{1,0:T(8,128)S(1)} all-gather(f32[8,4096]{1,0:T(8,128)} %reduce-scatter.8.cloned.1.call-done), channel_id=1, replica_groups=mesh['rep'=4,'tp'=8] {'rep'}, dimensions={1}, use_global_device_ids=true | all-gather | bytes 655360 | tf_op jit(solution)/shard_map/all_gather | solution.py:97
  296.5 9.5 %all_to_all.107 = bf16[8,8,2048]{2,0,1:T(8,128)(2,1)S(1)} all-to-all(bf16[8,8,2048]{2,0,1:T(8,128)(2,1)S(1)} %bitcast.118), channel_id=1, replica_groups=mesh['rep'=4,'tp'=8] {'tp'}, dimensions={1} | all-to-all | bytes 524288 | tf_op jit(solution)/shard_map/all_to_all | solution.py:90
  305.9 9.8 %fusion.14 = f32[64,4096]{1,0:T(8,128)} fusion(bf16[2048,4096]{1,0:T(8,128)(2,1)} %param.19, bf16[8,8,2048]{2,0,1:T(8,128)(2,1)S(1)} %all_to_all.107), kind=kOutput, calls=%fused_computation.45 | convolution fusion | flops 1073741824 | bytes 18087936 | tf_op jit(solution)/shard_map/dot_general | solution.py:92
  315.8 36.0 %reduce-scatter.10.cloned.1.call-done = f32[8,4096]{1,0:T(8,128)} async-done(((f32[64,4096]{1,0:T(8,128)}), f32[8,4096]{1,0:T(8,128)}) %reduce-scatter.10.cloned.1.call-update) | async-done | bytes 131088 | tf_op jit(solution)/shard_map/reduce_scatter | solution.py:91
  351.8 15.8 %all_gather.21 = f32[8,16384]{1,0:T(8,128)S(1)} all-gather(f32[8,4096]{1,0:T(8,128)} %reduce-scatter.10.cloned.1.call-done), channel_id=1, replica_groups=mesh['rep'=4,'tp'=8] {'rep'}, dimensions={1}, use_global_device_ids=true | all-gather | bytes 655360 | tf_op jit(solution)/shard_map/all_gather | solution.py:97
  368.0 9.5 %all_to_all.108 = bf16[8,8,2048]{2,0,1:T(8,128)(2,1)S(1)} all-to-all(bf16[8,8,2048]{2,0,1:T(8,128)(2,1)S(1)} %bitcast.119), channel_id=1, replica_groups=mesh['rep'=4,'tp'=8] {'tp'}, dimensions={1} | all-to-all | bytes 524288 | tf_op jit(solution)/shard_map/all_to_all | solution.py:90
  377.5 9.8 %fusion.12 = f32[64,4096]{1,0:T(8,128)} fusion(bf16[2048,4096]{1,0:T(8,128)(2,1)} %param.19, bf16[8,8,2048]{2,0,1:T(8,128)(2,1)S(1)} %all_to_all.108), kind=kOutput, calls=%fused_computation.43 | convolution fusion | flops 1073741824 | bytes 18087936 | tf_op jit(solution)/shard_map/dot_general | solution.py:92
  387.4 36.0 %reduce-scatter.12.cloned.1.call-done = f32[8,4096]{1,0:T(8,128)} async-done(((f32[64,4096]{1,0:T(8,128)}), f32[8,4096]{1,0:T(8,128)}) %reduce-scatter.12.cloned.1.call-update) | async-done | bytes 131088 | tf_op jit(solution)/shard_map/reduce_scatter | solution.py:91
  423.4 15.8 %all_gather.22 = f32[8,16384]{1,0:T(8,128)S(1)} all-gather(f32[8,4096]{1,0:T(8,128)} %reduce-scatter.12.cloned.1.call-done), channel_id=1, replica_groups=mesh['rep'=4,'tp'=8] {'rep'}, dimensions={1}, use_global_device_ids=true | all-gather | bytes 655360 | tf_op jit(solution)/shard_map/all_gather | solution.py:97
  439.6 9.5 %all_to_all.109 = bf16[8,8,2048]{2,0,1:T(8,128)(2,1)S(1)} all-to-all(bf16[8,8,2048]{2,0,1:T(8,128)(2,1)S(1)} %bitcast.116), channel_id=1, replica_groups=mesh['rep'=4,'tp'=8] {'tp'}, dimensions={1} | all-to-all | bytes 524288 | tf_op jit(solution)/shard_map/all_to_all | solution.py:90
  449.1 9.8 %fusion.10 = f32[64,4096]{1,0:T(8,128)} fusion(bf16[2048,4096]{1,0:T(8,128)(2,1)} %param.19, bf16[8,8,2048]{2,0,1:T(8,128)(2,1)S(1)} %all_to_all.109), kind=kOutput, calls=%fused_computation.41 | convolution fusion | flops 1073741824 | bytes 18087936 | tf_op jit(solution)/shard_map/dot_general | solution.py:92
  459.8 35.1 %reduce-scatter.14.cloned.1.call-done = f32[8,4096]{1,0:T(8,128)} async-done(((f32[64,4096]{1,0:T(8,128)}), f32[8,4096]{1,0:T(8,128)}) %reduce-scatter.14.cloned.1.call-update) | async-done | bytes 131088 | tf_op jit(solution)/shard_map/reduce_scatter | solution.py:91
  494.9 15.8 %all_gather.23 = f32[8,16384]{1,0:T(8,128)S(1)} all-gather(f32[8,4096]{1,0:T(8,128)} %reduce-scatter.14.cloned.1.call-done), channel_id=1, replica_groups=mesh['rep'=4,'tp'=8] {'rep'}, dimensions={1}, use_global_device_ids=true | all-gather | bytes 655360 | tf_op jit(solution)/shard_map/all_gather | solution.py:97
  (58 shorter events, 17.2 us)
Async XLA Ops:
  7.2 119.3 %all-reduce.2.cloned.1.call-start = ((), (), s32[]{:S(2)}) async-start(), calls=%async_computation.11 | async-start | bytes 10485760 | tf_op jit(solution)/shard_map/psum | solution.py:71
  14.9 16.1 %copy-start.3 = (s32[16]{0:T(128)S(1)}, s32[16]{0:T(128)}, u32[]{:S(2)}) copy-start(s32[16]{0:T(128)} %param.16) | copy-start | bytes 196
  14.9 112.8 %copy-start.1 = (bf16[16,5,2048]{2,0,1:T(8,128)(2,1)S(1)}, bf16[16,5,2048]{2,0,1:T(8,128)(2,1)}, u32[]{:S(2)}) copy-start(bf16[16,5,2048]{2,0,1:T(8,128)(2,1)} %param.15) | copy-start | bytes 983044
  14.9 131.4 %copy-start = (bf16[8,5,16384]{2,0,1:T(8,128)(2,1)S(1)}, bf16[8,5,16384]{2,0,1:T(8,128)(2,1)}, u32[]{:S(2)}) copy-start(bf16[8,5,16384]{2,0,1:T(8,128)(2,1)} %param.17) | copy-start | bytes 3932164
  14.9 131.4 %copy-start.2 = (bf16[16384]{0:T(1024)(128)(2,1)S(1)}, bf16[16384]{0:T(1024)(128)(2,1)}, u32[]{:S(2)}) copy-start(bf16[16384]{0:T(1024)(128)(2,1)} %param.18) | copy-start | bytes 98308
  142.9 10.3 %all-to-all-start = ((bf16[8,8,2048]{2,1,0:T(8,128)(2,1)}), bf16[8,8,2048]{2,1,0:T(8,128)(2,1)S(1)}, u32[]{:S(2)}, u32[]{:S(2)}) async-start(bf16[8,8,2048]{2,1,0:T(8,128)(2,1)} %bitcast.14), calls=%async_computation | async-start | bytes 524288 | tf_op jit(solution)/shard_map/all_to_all | solution.py:83
  146.3 62.3 %reduce-scatter.6.cloned.1.call-start = ((), (), s32[]{:S(2)}) async-start(), calls=%async_computation.12 | async-start | bytes 1179648 | tf_op jit(solution)/shard_map/reduce_scatter | solution.py:91
  172.7 107.4 %reduce-scatter.8.cloned.1.call-start = ((), (), s32[]{:S(2)}) async-start(), calls=%async_computation.13 | async-start | bytes 1179648 | tf_op jit(solution)/shard_map/reduce_scatter | solution.py:91
  244.0 107.8 %reduce-scatter.10.cloned.1.call-start = ((), (), s32[]{:S(2)}) async-start(), calls=%async_computation.14 | async-start | bytes 1179648 | tf_op jit(solution)/shard_map/reduce_scatter | solution.py:91
  315.7 107.6 %reduce-scatter.12.cloned.1.call-start = ((), (), s32[]{:S(2)}) async-start(), calls=%async_computation.15 | async-start | bytes 1179648 | tf_op jit(solution)/shard_map/reduce_scatter | solution.py:91
  387.3 107.6 %reduce-scatter.14.cloned.1.call-start = ((), (), s32[]{:S(2)}) async-start(), calls=%async_computation.16 | async-start | bytes 1179648 | tf_op jit(solution)/shard_map/reduce_scatter | solution.py:91
Sparse Core Ops, SparseCore 0:
  31.1 95.2 all-reduce.1
  172.8 35.6 reduce-scatter.5
  244.1 35.9 reduce-scatter.7
  315.9 35.9 reduce-scatter.9
  387.4 35.8 reduce-scatter.11
  459.0 35.9 reduce-scatter.13
where the time goes:
time: 519 us; the launch traced here: 518 us
  waiting for transfers between devices  281 us (54%)
  blocking collectives  141 us (27%)
  matrix products  69.4 us (13%)
  between operations  14.4 us (3%)
    reduce_scatter x5, waiting for transfers between devices, local(): lax.psum_scatter(jnp.dot(input_cols, draft_proj, preferred_element_type=j...  179 us
    psum x1, waiting for transfers between devices, local(): summed = lax.psum(projected, 'tp')  95.4 us
    all_gather x5, blocking collectives, local(): update = lax.all_gather(own_update, 'rep', axis=1, tiled=True)  79.1 us
    dot_general x5, matrix products, local(): jnp.dot(input_cols, draft_proj, preferred_element_type=jnp.float32)  48.9 us
    all_to_all x5, blocking collectives, local(): lax.all_to_all(normed, 'tp', split_axis=1, concat_axis=0, tiled=True)  47.2 us
    dot_general x1, matrix products, local(): jnp.dot(attn.reshape(row_count * draft_len, width), out_proj, preferred_e...  16 us
    all_gather x1, blocking collectives, local(): every_row = lax.all_gather(feature, 'rep', axis=0, tiled=True)  14.6 us
  transfers between devices with their start and end apart: 7, of which 7 were waited for; matrix products, arithmetic and copies ran while one was open for 0% of the time, Pallas kernels for 0%

commit v1 on v0

v1 whole, which is shorter than its diff:
```python
import functools

import jax
import jax.numpy as jnp
from jax import lax
from jax.experimental import pallas as pl
from jax.experimental.pallas import tpu as pltpu
from jax.sharding import PartitionSpec as P

KV_HEADS = 4
HEAD_DIM = 128
MESH = pl.DeviceIdType.MESH
F32 = jnp.float32
BF16 = jnp.bfloat16
EXACT = lax.Precision.HIGHEST


def attend(queries, cache_keys, cache_vals, fresh_keys, fresh_vals, cache_len):
    row_count, draft_len, width = queries.shape
    group = width // HEAD_DIM
    scale = HEAD_DIM ** (-0.5)
    query_all = queries.reshape(row_count, draft_len, group, HEAD_DIM)
    cache_scores = (
        jnp.einsum("rjgd,rpd->rjgp", query_all, cache_keys, preferred_element_type=F32) * scale
    )
    positions = jnp.arange(cache_keys.shape[1], dtype=jnp.int32)
    valid = positions[None, :] < cache_len[:, None]
    cache_scores = jnp.where(valid[:, None, None, :], cache_scores, -jnp.inf)
    fresh_scores = (
        jnp.einsum("rjgd,rid->rjgi", query_all, fresh_keys, preferred_element_type=F32) * scale
    )
    causal = jnp.arange(draft_len)[None, :] <= jnp.arange(draft_len)[:, None]
    fresh_scores = jnp.where(causal[None, :, None, :], fresh_scores, -jnp.inf)
    highest = jnp.maximum(jnp.max(cache_scores, -1), jnp.max(fresh_scores, -1))[..., None]
    cache_exp = jnp.exp(cache_scores - highest)
    fresh_exp = jnp.exp(fresh_scores - highest)
    total = jnp.sum(cache_exp, -1, keepdims=True) + jnp.sum(fresh_exp, -1, keepdims=True)
    cache_weights = (cache_exp / total).astype(BF16)
    fresh_weights = (fresh_exp / total).astype(BF16)
    mixed = jnp.einsum("rjgp,rpd->rjgd", cache_weights, cache_vals, preferred_element_type=F32)
    mixed = mixed + jnp.einsum(
        "rjgi,rid->rjgd", fresh_weights, fresh_vals, preferred_element_type=F32
    )
    return mixed.reshape(row_count, draft_len, width).astype(BF16)


def fused(
    T,
    R,
    STEPS,
    attn_ref,
    acc_ref,
    resid_ref,
    racc_ref,
    gain_ref,
    emb_ref,
    oproj_ref,
    dproj_ref,
    ver_ref,
    out_ref,
    w_buf,
    wo_buf,
    ws_buf,
    emb_in,
    emb_f,
    acc_in,
    racc_in,
    part,
    state,
    rs_out,
    rs_in,
    sq_out,
    sq_in,
    z_buf,
    x_buf,
    f_out,
    f_in,
    g_buf,
    v_out,
    v_in,
    w_sem,
    wo_sem,
    ws_sem,
    e_send,
    e_recv,
    a_send,
    a_recv,
    ra_send,
    ra_recv,
    rs_send,
    rs_recv,
    sq_send,
    sq_recv,
    z_send,
    z_recv,
    x_send,
    x_recv,
    f_send,
    f_recv,
    g_send,
    g_recv,
    v_send,
    v_recv,
):
    t = lax.axis_index("tp")
    r = lax.axis_index("rep")
    ratio = T // R
    rows, cw = state.shape
    width = gain_ref.shape[1]
    kb = width // T
    nb = width // R
    own_rows = rows // T
    rr = acc_ref.shape[0]

    def plane(k):
        return lax.rem(t + k, T)

    def tower(j):
        return lax.rem(r + j, R)

    def tower_back(j):
        return lax.rem(r - j + R, R)

    def remote(src, dst, send, recv, axis, index):
        return pltpu.make_async_remote_copy(
            src_ref=src,
            dst_ref=dst,
            send_sem=send,
            recv_sem=recv,
            device_id={axis: index},
            device_id_type=MESH,
        )

    def cols(start, size):
        return pl.ds(pl.multiple_of(start, 128), size)

    wo_copy = pltpu.make_async_copy(oproj_ref.at[:, cols(r * nb, nb)], wo_buf, wo_sem)
    wo_copy.start()

    def ws_copy(kk, slot):
        return pltpu.make_async_copy(
            oproj_ref.at[:, cols(plane(kk + 1) * kb, kb)], ws_buf.at[slot], ws_sem.at[slot]
        )

    barrier = pltpu.get_barrier_semaphore()
    for k in range(1, T):
        pl.semaphore_signal(barrier, inc=1, device_id={"tp": plane(k)}, device_id_type=MESH)
    for j in range(1, R):
        pl.semaphore_signal(barrier, inc=1, device_id={"rep": tower(j)}, device_id_type=MESH)
    pl.semaphore_wait(barrier, T - 1 + R - 1)

    def a_copy(j):
        return remote(acc_ref, acc_in.at[r], a_send.at[j], a_recv.at[j], "rep", tower(j))

    for j in range(1, R):
        a_copy(j).start()
    acc_in[r] = acc_ref[...]

    home = t // ratio
    ra_offset = lax.rem(home - r + R, R)

    def ra_copy():
        return remote(racc_ref, racc_in.at[r], ra_send, ra_recv.at[ra_offset], "rep", home)

    @pl.when(home != r)
    def _():
        ra_copy().start()

    @pl.when(home == r)
    def _():
        racc_in[r] = racc_ref[...]

    w_copy = pltpu.make_async_copy(dproj_ref, w_buf, w_sem)
    w_copy.start()

    def e_copy(k):
        return remote(
            emb_ref.at[:, cols((r * T + plane(k)) * cw, cw)],
            emb_in.at[k],
            e_send.at[k],
            e_recv.at[k],
            "tp",
            plane(k),
        )

    e_own = pltpu.make_async_copy(
        emb_ref.at[:, cols((r * T + t) * cw, cw)], emb_in.at[0], e_send.at[0]
    )
    e_own.start()

    for k in range(1, T):
        e_copy(k).start()
    ws_copy(0, 0).start()
    ws_copy(1, 1).start()

    for j in range(1, R):
        a_copy(j).wait_recv()

    @pl.when(home == r)
    def _():
        for j in range(1, R):
            remote(
                racc_ref, racc_in.at[tower_back(j)], ra_send, ra_recv.at[j], "rep", tower(j)
            ).wait_recv()

    wo_copy.wait()

    def rs_copy(i, k):
        return remote(
            rs_out.at[k], rs_in.at[i, k], rs_send.at[k], rs_recv.at[i, k], "tp", plane(k)
        )

    def finish(i):
        for k in range(1, T):
            rs_copy(i, k).wait_recv()
        total = rs_in[i, 0].astype(F32)
        for k in range(1, T):
            total = total + rs_in[i, k].astype(F32)
        for k in range(1, T):
            rs_copy(i, k).wait_send()
        return total

    first = acc_in[...].reshape(rows, acc_ref.shape[1])

    def project(kk, _):
        k = lax.rem(kk + 1, T)
        c = plane(k)
        part[...] = jnp.dot(first, wo_buf[:, cols(c * cw, cw)], preferred_element_type=F32)

        @pl.when(r * ratio + c // R == t)
        def _():
            part[...] += (
                racc_in[:, :, cols(lax.rem(c, R) * cw, cw)].reshape(rows, cw).astype(F32)
            )

        @pl.when(kk < T - 1)
        def _():
            rs_out[k] = part[...].astype(BF16)
            rs_copy(0, k).start()

        @pl.when(kk == T - 1)
        def _():
            rs_in[0, 0] = part[...].astype(BF16)

        return 0

    lax.fori_loop(0, T, project, 0)

    e_own.wait()
    for k in range(1, T):
        e_copy(k).wait_recv()

    def place(k, _):
        source = lax.rem(t - k + T, T)
        block = emb_in[k].astype(F32)
        for s in range(STEPS):
            emb_f[s, pl.ds(pl.multiple_of(source * own_rows, own_rows), own_rows), :] = block[
                s * own_rows : (s + 1) * own_rows
            ]
        return 0

    lax.fori_loop(0, T, place, 0)
    state[...] = finish(0).astype(BF16).astype(F32)
    w_copy.wait()

    gain_own = gain_ref[:, cols((r * T + t) * cw, cw)]
    gain_back = 1.0 / gain_ref[:, cols(t * kb, kb)]

    vb = min(kb, 512)

    def v_copy(kk):
        return remote(
            v_out.at[kk], v_in.at[kk], v_send.at[kk], v_recv.at[kk], "tp", plane(kk + 1)
        )

    def v_chunk(kk):
        slot = lax.rem(kk, 2)
        ws_copy(kk, slot).wait()

        def block(b, _):
            here = cols(b * vb, vb)
            v_out[kk, :, here] = jnp.dot(
                attn_ref[...], ws_buf[slot, :, here], preferred_element_type=F32
            ).astype(BF16)
            return 0

        lax.fori_loop(0, kb // vb, block, 0)

        @pl.when(kk < T - 1)
        def _():
            v_copy(kk).start()

        @pl.when(kk < T - 2)
        def _():
            ws_copy(kk + 2, slot).start()

    gaps = 2 * (STEPS - 1)
    per_gap = -(-T // gaps)

    def v_gap(g):
        for n in range(per_gap):
            kk = g * per_gap + n

            @pl.when(kk < T)
            def _():
                v_chunk(kk)

    def x_copy(s, j):
        q = tower_back(j)
        target = q * ratio + t // R
        m = lax.rem(t, R)
        return target, remote(
            z_buf.at[s, q], x_buf.at[s, m], x_send.at[j], x_recv.at[s, m], "tp", target
        )

    def z_copy(s, j):
        return remote(z_buf.at[s, r], z_buf.at[s, r], z_send.at[j], z_recv.at[s, j], "rep", tower(j))

    def z_arrival(s, j):
        q = tower_back(j)
        return remote(z_buf.at[s, q], z_buf.at[s, q], z_send.at[j], z_recv.at[s, j], "rep", tower(j))

    def sq_copy(s, k):
        return remote(
            sq_out, sq_in.at[s, k], sq_send.at[k], sq_recv.at[s, k], "tp", plane(k)
        )

    def step(s, _):
        mixed = state[...] + emb_f[s]
        z_buf[s, r] = (mixed * gain_own).astype(BF16)
        for j in range(1, R):
            z_copy(s, j).start()
        for j in range(R):
            if j == 1:
                v_gap(2 * s)
            if j > 0:
                z_arrival(s, j).wait_recv()
            target, copy = x_copy(s, j)

            @pl.when(target != t)
            def _():
                copy.start()

            @pl.when(target == t)
            def _():
                x_buf[s, lax.rem(t, R)] = z_buf[s, tower_back(j)]

        for m in range(R):
            source = lax.rem(t, ratio) * R + m

            @pl.when(source != t)
            def _():
                remote(
                    z_buf.at[s, 0], x_buf.at[s, m], x_send.at[0], x_recv.at[s, m], "tp", source
                ).wait_recv()

        x = jnp.concatenate([x_buf[s, m] for m in range(R)], axis=1)
        plain = x.astype(F32) * gain_back
        plain = plain * plain
        lanes = plain[:, :128]
        for b in range(1, kb // 128):
            lanes = lanes + plain[:, b * 128 : (b + 1) * 128]
        sq_out[:, :rows] = lax.dot_general(
            jnp.ones((8, 128), F32),
            lanes,
            (((1,), (1,)), ((), ())),
            precision=EXACT,
            preferred_element_type=F32,
        )
        for k in range(1, T):
            sq_copy(s, k).start()
        sq_in[s, 0] = sq_out[...]

        def multiply(kk, _):
            k = lax.rem(kk + 1, T)
            product = jnp.dot(
                x, w_buf[:, cols(plane(k) * cw, cw)], preferred_element_type=F32
            ).astype(BF16)

            @pl.when(kk < T - 1)
            def _():
                rs_out[k] = product
                rs_copy(s + 1, k).start()

            @pl.when(kk == T - 1)
            def _():
                rs_in[s + 1, 0] = product

            return 0

        lax.fori_loop(0, T, multiply, 0)
        v_gap(2 * s + 1)
        for k in range(1, T):
            sq_copy(s, k).wait_recv()
        squares = sq_in[s, 0]
        for k in range(1, T):
            squares = squares + sq_in[s, k]
        column = lax.dot_general(
            squares,
            jnp.full((8, 128), 0.125, F32),
            (((0,), (0,)), ((), ())),
            precision=EXACT,
            preferred_element_type=F32,
        )[:rows, :1]
        inverse = lax.rsqrt(column / width + 1e-05)
        update = finish(s + 1) * inverse
        state[...] += update / (1.0 + jnp.exp(-update))
        for k in range(1, T):
            sq_copy(s, k).wait_send()
        for j in range(1, R):
            z_copy(s, j).wait_send()
        for j in range(R):
            target, copy = x_copy(s, j)

            @pl.when(target != t)
            def _():
                copy.wait_send()

        return 0

    sq_out[...] = jnp.zeros_like(sq_out)
    lax.fori_loop(0, STEPS, step, 0)

    def f_copy(k):
        return remote(f_out.at[k], f_in.at[t], f_send.at[k], f_recv.at[k], "tp", plane(k))

    blank = jnp.zeros((16 - own_rows, cw), F32)
    for k in range(T):
        here = pl.ds(pl.multiple_of(plane(k) * own_rows, own_rows), own_rows)
        f_out[k] = jnp.concatenate([state[here, :], blank], axis=0).astype(BF16)
        if k > 0:
            f_copy(k).start()
    f_in[t] = f_out[0]

    def v_wait(kk, _):
        remote(
            v_out.at[kk], v_in.at[kk], v_send.at[kk], v_recv.at[kk], "tp", plane(kk + 1)
        ).wait()
        return 0

    for k in range(1, T):
        remote(
            f_out.at[k],
            f_in.at[lax.rem(t - k + T, T)],
            f_send.at[k],
            f_recv.at[k],
            "tp",
            plane(k),
        ).wait()
    half = T // 2
    for k in range(half):
        top = f_in[k].astype(F32)[:own_rows]
        low = f_in[k + half].astype(F32)[:own_rows]
        g_buf[r, :, k * cw : (k + 1) * cw] = jnp.concatenate([top, low], axis=0).astype(BF16)

    def g_copy(j):
        return remote(g_buf.at[r], g_buf.at[r], g_send.at[j], g_recv.at[j], "rep", tower(j))

    for j in range(1, R):
        g_copy(j).start()

    lax.fori_loop(0, T - 1, v_wait, 0)

    def v_sum(b, _):
        here = cols(b * vb, vb)
        total = v_out[T - 1, :, here].astype(F32)
        for kk in range(T - 1):
            total = total + v_in[kk, :, here].astype(F32)
        ver_ref[:, here] = (resid_ref[:, here].astype(F32) + total).astype(BF16)
        return 0

    lax.fori_loop(0, kb // vb, v_sum, 0)

    for j in range(1, R):
        q = tower_back(j)
        remote(g_buf.at[q], g_buf.at[q], g_send.at[j], g_recv.at[j], "rep", tower(j)).wait()
    for q in range(R):
        block = g_buf[q].astype(F32)
        out_ref[:, q * nb : q * nb + nb // 2] = block[:own_rows].astype(BF16)
        out_ref[:, q * nb + nb // 2 : (q + 1) * nb] = block[own_rows:].astype(BF16)

    for j in range(1, R):
        a_copy(j).wait_send()

    @pl.when(home != r)
    def _():
        ra_copy().wait_send()

    for k in range(1, T):
        e_copy(k).wait_send()


def local(
    T,
    R,
    queries,
    kv_cache,
    kv_new,
    cache_len,
    out_proj,
    residual,
    accepted,
    draft_emb,
    draft_gain,
    draft_proj,
):
    row_count, draft_len, kdim = queries.shape
    width = draft_gain.shape[0]
    rows = row_count * R
    own_rows, steps = draft_emb.shape[:2]
    cw = width // (T * R)
    kb = width // T
    nb = width // R
    group = kdim * T // HEAD_DIM // KV_HEADS
    kv_start = lax.axis_index("tp") * (kdim // HEAD_DIM) // group * HEAD_DIM
    own_cache = lax.dynamic_slice_in_dim(kv_cache, kv_start, HEAD_DIM, 3)
    own_fresh = lax.dynamic_slice_in_dim(kv_new, kv_start, HEAD_DIM, 3)
    attn = attend(
        queries, own_cache[:, 0], own_cache[:, 1], own_fresh[:, 0], own_fresh[:, 1], cache_len
    )
    picked = (jnp.arange(draft_len, dtype=jnp.int32)[None, :] == accepted[:, None])[:, :, None]

    def pick(array):
        return jnp.sum(jnp.where(picked, array.astype(F32), 0.0), axis=1).astype(BF16)

    emb = draft_emb.transpose(1, 0, 2).reshape(steps * own_rows, width)
    emb_rows = -(-steps * own_rows // 16) * 16
    emb = jnp.pad(emb, ((0, emb_rows - steps * own_rows), (0, 0)))
    token_rows = row_count * draft_len
    dma = pltpu.SemaphoreType.DMA
    vmem = pl.BlockSpec(memory_space=pltpu.VMEM)
    hbm = pl.BlockSpec(memory_space=pl.ANY)
    verified, features = pl.pallas_call(
        functools.partial(fused, T, R, steps),
        out_shape=(
            jax.ShapeDtypeStruct((token_rows, kb), BF16),
            jax.ShapeDtypeStruct((own_rows, width), BF16),
        ),
        in_specs=[vmem] * 5 + [hbm] * 3,
        out_specs=(vmem, vmem),
        scratch_shapes=[
            pltpu.VMEM((kb, nb), BF16),
            pltpu.VMEM((kdim, nb), BF16),
            pltpu.VMEM((2, kdim, kb), BF16),
            pltpu.VMEM((T, emb_rows, cw), BF16),
            pltpu.VMEM((steps, rows, cw), F32),
            pltpu.VMEM((R, row_count, kdim), BF16),
            pltpu.VMEM((R, row_count, kb), BF16),
            pltpu.VMEM((rows, cw), F32),
            pltpu.VMEM((rows, cw), F32),
            pltpu.VMEM((T, rows, cw), BF16),
            pltpu.VMEM((steps + 1, T, rows, cw), BF16),
            pltpu.VMEM((8, 128), F32),
            pltpu.VMEM((steps, T, 8, 128), F32),
            pltpu.VMEM((steps, R, rows, cw), BF16),
            pltpu.VMEM((steps, R, rows, cw), BF16),
            pltpu.VMEM((T, 16, cw), BF16),
            pltpu.VMEM((T, 16, cw), BF16),
            pltpu.VMEM((R, 16, nb // 2), BF16),
            pltpu.VMEM((T, token_rows, kb), BF16),
            pltpu.VMEM((T, token_rows, kb), BF16),
            dma,
            dma,
            dma((2,)),
            dma((T,)),
            dma((T,)),
            dma((R,)),
            dma((R,)),
            dma,
            dma((R,)),
            dma((T,)),
            dma((steps + 1, T)),
            dma((T,)),
            dma((steps, T)),
            dma((R,)),
            dma((steps, R)),
            dma((R,)),
            dma((steps, R)),
            dma((T,)),
            dma((T,)),
            dma((R,)),
            dma((R,)),
            dma((T,)),
            dma((T,)),
        ],
        compiler_params=pltpu.CompilerParams(
            collective_id=0, has_side_effects=True, vmem_limit_bytes=56 * 2**20
        ),
        name="verify_and_draft",
    )(
        attn.reshape(token_rows, kdim),
        pick(attn),
        residual.reshape(token_rows, kb),
        pick(residual),
        draft_gain.astype(F32).reshape(1, width),
        emb,
        out_proj,
        draft_proj,
    )
    return verified.reshape(row_count, draft_len, kb), features


def solution(mesh):
    in_specs = (
        P("rep", None, "tp"),
        P("rep", None, None, None),
        P("rep", None, None, None),
        P("rep"),
        P("tp", None),
        P("rep", None, "tp"),
        P("rep"),
        P("tp", None, None),
        P(),
        P("tp", "rep"),
    )
    out_specs = (P("rep", None, "tp"), P("tp", None))
    body = functools.partial(local, mesh.shape["tp"], mesh.shape["rep"])
    return jax.shard_map(body, mesh=mesh, in_specs=in_specs, out_specs=out_specs, check_vma=False)
```

time: 519 us -> 175 us (0.34)
  waiting for transfers between devices: 281 us -> 0 us
  Pallas kernels: 0 us -> 154 us
  blocking collectives: 141 us -> 0 us
  matrix products: 69.4 us -> 4.45 us
  between operations: 14.4 us -> 0.74 us
  local copies, waits for them, and re-layouts: 4.17 us -> 10.3 us
    reduce_scatter x5 -> x0, waiting for transfers between devices: 179 us -> none  [local(): lax.psum_scatter(jnp.dot(input_cols, draft_proj, preferred_element_type=j...]
    pallas_call x0 -> x1, Pallas kernels: none -> 154 us  [local(): pl.pallas_call(functools.partial(fused, T, R, steps), out_shape=(jax.Shap...]
    psum x1 -> x0, waiting for transfers between devices: 95.4 us -> none  [local(): summed = lax.psum(projected, 'tp')]
    all_gather x6 -> x0, blocking collectives: 93.7 us -> none  [the longest x5 79.1 us: local(): update = lax.all_gather(own_update, 'rep', axis=1, tiled=True)]
    dot_general x6 -> x0, matrix products: 64.9 us -> none  [the longest x5 48.9 us: local(): jnp.dot(input_cols, draft_proj, preferred_element_type=jnp.float32)]
    all_to_all x5 -> x0, blocking collectives: 47.2 us -> none  [local(): lax.all_to_all(normed, 'tp', split_axis=1, concat_axis=0, tiled=True)]
    all_to_all x1 -> x0, waiting for transfers between devices: 6.74 us -> none  [local(): lax.all_to_all(every_row, 'tp', split_axis=0, concat_axis=1, tiled=True)]
  transfers between devices with their start and end apart: 7 -> 0, of which waited for: 7 -> 0; matrix products, arithmetic and copies ran while one was open for 0% -> 0% of each run, Pallas kernels for 0% -> 0%
where the time goes in v1:
time: 175 us
  Pallas kernels  154 us (88%)
  local copies, waits for them, and re-layouts  10.3 us (6%)
  other arithmetic  5.16 us (3%)
  matrix products  4.45 us (3%)
    pallas_call x1, Pallas kernels, local(): pl.pallas_call(functools.partial(fused, T, R, steps), out_shape=(jax.Shap...  154 us
    unnamed x8, local copies, waits for them, and re-layouts  6.02 us

profile of v1, /device:TPU:0, one launch (start us, length us, event | category | flops | bytes accessed | tf_op | source)
XLA Modules:
  0.0 174.6 jit_solution(10902346085974730319)
XLA Ops:
  0.6 0.0 copy-start
  0.7 0.8 iota_compare_fusion.1
  1.5 0.1 copy.26
  1.6 0.7 iota_compare_fusion
  2.3 1.8 %select_reduce_fusion.racc_ref = bf16[16,2048]{1,0:T(8,128)(2,1)} fusion(bf16[16,5,2048]{2,0,1:T(8,128)(2,1)} %param.15, pred[16,5]{0,1:T(8,128)(4,1)S(1)} %copy.26), kind=kLoop, calls=%fused_computation.11 | loop fusion | flops 458752 | bytes 393296 | tf_op jit(solution)/shard_map/reduce_sum | solution.py:524
  4.1 1.4 reshape.94
  5.5 1.0 constant_dynamic-slice_fusion.1
  6.4 0.9 copy.39
  7.4 0.7 fusion.17
  8.1 1.2 copy.25
  9.3 0.9 reshape.89.resid_ref
  10.2 1.8 %fusion.16 = (f32[16,5,8]{2,1,0:T(8,128)S(1)}, f32[16,5,8,256]{3,2,1,0:T(8,128)S(1)}) fusion(bf16[16,5,8,128]{3,2,0,1:T(8,128)(2,1)S(1)} %bitcast.60, bf16[16,2,256,512]{3,2,1,0:T(8,128)(2,1)} %param.11, s32[]{:T(128)S(6)} %select_n.30, pred[16,256]{1,0:T(8,128)(4,1)S(1)} %iota_compare_fusion), kind=kOutput, calls=%fused_computation.36 | convolution fusion | flops 42433920 | bytes 1874436 | tf_op jit(solution)/shard_map/rjgd,rpd->rjgp/dot_general | solution.py:24
  12.0 0.1 fusion.9
  12.1 0.3 fusion.6
  12.4 1.6 fusion.5
  14.1 0.3 select_reduce_fusion.1
  14.4 0.6 copy.61
  15.0 0.7 copy.60
  15.7 0.0 copy-done
  15.7 1.3 pad.4.emb_ref
  17.0 154.0 %verify_and_draft.1 = (bf16[80,2048]{1,0:T(8,128)(2,1)}, bf16[8,16384]{1,0:T(8,128)(2,1)}) custom-call(bf16[80,1024]{1,0:T(8,128)(2,1)} %bitcast.62, bf16[16,1024]{1,0:T(8,128)(2,1)} %bitcast.66, bf16[80,2048]{1,0:T(8,128)(2,1)} %reshape.89.resid_ref, bf16[16,2048]{1,0:T(8,128)(2,1)} %select_reduce_fusion.racc_ref, f32[1,16384]{1,0:T(1,128)} %bitcast.63, ...), custom_call_target="tpu_custom_call" | custom-call | tf_op jit(solution)/shard_map/verify_and_draft/pallas_call | solution.py:533
  170.9 1.1 reshape.93
  172.0 0.9 copy.27
  173.0 1.7 copy.63
  (3 shorter events, 0.0 us)
Async XLA Ops:
  0.6 15.1 %copy-start = (bf16[8,5,16384]{2,0,1:T(8,128)(2,1)S(1)}, bf16[8,5,16384]{2,0,1:T(8,128)(2,1)}, u32[]{:S(2)}) copy-start(bf16[8,5,16384]{2,0,1:T(8,128)(2,1)} %param.17) | copy-start | bytes 3932164

commit v2 on v1

--- a/solution.py
+++ b/solution.py
@@ -15,49 +15,28 @@
 EXACT = lax.Precision.HIGHEST
 
 
-def attend(queries, cache_keys, cache_vals, fresh_keys, fresh_vals, cache_len):
-    row_count, draft_len, width = queries.shape
-    group = width // HEAD_DIM
-    scale = HEAD_DIM ** (-0.5)
-    query_all = queries.reshape(row_count, draft_len, group, HEAD_DIM)
-    cache_scores = (
-        jnp.einsum("rjgd,rpd->rjgp", query_all, cache_keys, preferred_element_type=F32) * scale
-    )
-    positions = jnp.arange(cache_keys.shape[1], dtype=jnp.int32)
-    valid = positions[None, :] < cache_len[:, None]
-    cache_scores = jnp.where(valid[:, None, None, :], cache_scores, -jnp.inf)
-    fresh_scores = (
-        jnp.einsum("rjgd,rid->rjgi", query_all, fresh_keys, preferred_element_type=F32) * scale
-    )
-    causal = jnp.arange(draft_len)[None, :] <= jnp.arange(draft_len)[:, None]
-    fresh_scores = jnp.where(causal[None, :, None, :], fresh_scores, -jnp.inf)
-    highest = jnp.maximum(jnp.max(cache_scores, -1), jnp.max(fresh_scores, -1))[..., None]
-    cache_exp = jnp.exp(cache_scores - highest)
-    fresh_exp = jnp.exp(fresh_scores - highest)
-    total = jnp.sum(cache_exp, -1, keepdims=True) + jnp.sum(fresh_exp, -1, keepdims=True)
-    cache_weights = (cache_exp / total).astype(BF16)
-    fresh_weights = (fresh_exp / total).astype(BF16)
-    mixed = jnp.einsum("rjgp,rpd->rjgd", cache_weights, cache_vals, preferred_element_type=F32)
-    mixed = mixed + jnp.einsum(
-        "rjgi,rid->rjgd", fresh_weights, fresh_vals, preferred_element_type=F32
-    )
-    return mixed.reshape(row_count, draft_len, width).astype(BF16)
-
-
 def fused(
     T,
     R,
     STEPS,
-    attn_ref,
-    acc_ref,
+    len_ref,
+    pick_ref,
+    q_ref,
+    fresh_ref,
     resid_ref,
-    racc_ref,
     gain_ref,
+    kv_ref,
     emb_ref,
     oproj_ref,
     dproj_ref,
     ver_ref,
     out_ref,
+    kv_buf,
+    padded,
+    attn_ref,
+    acc_ref,
+    racc_f,
+    racc_ref,
     w_buf,
     wo_buf,
     ws_buf,
@@ -76,8 +55,11 @@
     f_out,
     f_in,
     g_buf,
+    p_out,
+    p_in,
     v_out,
     v_in,
+    kv_sem,
     w_sem,
     wo_sem,
     ws_sem,
@@ -99,6 +81,8 @@
     f_recv,
     g_send,
     g_recv,
+    p_send,
+    p_recv,
     v_send,
     v_recv,
 ):
@@ -110,10 +94,22 @@
     kb = width // T
     nb = width // R
     own_rows = rows // T
-    rr = acc_ref.shape[0]
+    rr, draft_len, kdim = q_ref.shape
+    heads = kdim // HEAD_DIM
+    chips = T // 2
+    core = lax.rem(t, 2)
+    chip = t // 2
+    halves, hw = x_buf.shape[1] // R, x_buf.shape[3]
 
     def plane(k):
         return lax.rem(t + k, T)
+
+    def flip(index, k, limit):
+        out, bit = 0, 1
+        while bit < limit:
+            out = out + bit * lax.rem(index // bit + k // bit, 2)
+            bit *= 2
+        return out
 
     def tower(j):
         return lax.rem(r + j, R)
@@ -134,13 +130,35 @@
     def cols(start, size):
         return pl.ds(pl.multiple_of(start, 128), size)
 
+    kv_group = t * heads // (heads * T // KV_HEADS)
+    kv_copy = pltpu.make_async_copy(
+        kv_ref.at[:, :, :, cols(kv_group * HEAD_DIM, HEAD_DIM)], kv_buf, kv_sem
+    )
+    kv_copy.start()
     wo_copy = pltpu.make_async_copy(oproj_ref.at[:, cols(r * nb, nb)], wo_buf, wo_sem)
     wo_copy.start()
 
-    def ws_copy(kk, slot):
+    def turn(n, own):
+        k = chips - 1 - n
+        swapped = (k // 4) * 4 + lax.rem(k, 2) * 2 + lax.rem(k // 2, 2)
+        return k + (core if own else 1 - core) * (swapped - k)
+
+    def served(n, own):
+        return flip(chip, turn(n, own), chips) * 2 + (core if own else 1 - core)
+
+    def ws_copy(n, own):
         return pltpu.make_async_copy(
-            oproj_ref.at[:, cols(plane(kk + 1) * kb, kb)], ws_buf.at[slot], ws_sem.at[slot]
-        )
+            oproj_ref.at[:, cols(served(n, own) * kb, kb)], ws_buf.at[own], ws_sem.at[own]
+        )
+
+    def pick_row(n, _):
+        block = resid_ref[n].astype(F32)
+        chosen = lax.broadcasted_iota(jnp.int32, block.shape, 0) == pick_ref[n]
+        racc_f[pl.ds(n, 1), :] = jnp.sum(jnp.where(chosen, block, 0.0), axis=0, keepdims=True)
+        return 0
+
+    lax.fori_loop(0, rr, pick_row, 0)
+    racc_ref[...] = racc_f[...].astype(BF16)
 
     barrier = pltpu.get_barrier_semaphore()
     for k in range(1, T):
@@ -148,13 +166,6 @@
     for j in range(1, R):
         pl.semaphore_signal(barrier, inc=1, device_id={"rep": tower(j)}, device_id_type=MESH)
     pl.semaphore_wait(barrier, T - 1 + R - 1)
-
-    def a_copy(j):
-        return remote(acc_ref, acc_in.at[r], a_send.at[j], a_recv.at[j], "rep", tower(j))
-
-    for j in range(1, R):
-        a_copy(j).start()
-    acc_in[r] = acc_ref[...]
 
     home = t // ratio
     ra_offset = lax.rem(home - r + R, R)
@@ -191,7 +202,84 @@
     for k in range(1, T):
         e_copy(k).start()
     ws_copy(0, 0).start()
-    ws_copy(1, 1).start()
+    ws_copy(0, 1).start()
+
+    kv_copy.wait()
+    tall = 8 * heads
+    scale = HEAD_DIM ** (-0.5)
+    token = lax.rem(lax.broadcasted_iota(jnp.int32, (tall, 128), 0), 8)
+    fresh_ok = lax.broadcasted_iota(jnp.int32, (tall, 128), 1) <= token
+    slots = kv_buf.shape[2]
+    slot_at = lax.broadcasted_iota(jnp.int32, (tall, slots), 1)
+    across = (((1,), (1,)), ((), ()))
+    fresh_cols = cols(kv_group * HEAD_DIM, HEAD_DIM)
+    empty = jnp.zeros((8 - draft_len, kdim), F32)
+    unused = jnp.zeros((128 - draft_len, HEAD_DIM), F32)
+
+    def attend_row(n, _):
+        query = jnp.concatenate([q_ref[n].astype(F32), empty], axis=0)
+        query = jnp.concatenate(
+            [query[:, h * HEAD_DIM : (h + 1) * HEAD_DIM] for h in range(heads)], axis=0
+        ).astype(BF16)
+        fresh_keys = jnp.concatenate(
+            [fresh_ref[n, 0, :, fresh_cols].astype(F32), unused], axis=0
+        ).astype(BF16)
+        fresh_vals = jnp.concatenate(
+            [fresh_ref[n, 1, :, fresh_cols].astype(F32), unused], axis=0
+        ).astype(BF16)
+        cache_scores = (
+            lax.dot_general(query, kv_buf[n, 0], across, preferred_element_type=F32) * scale
+        )
+        fresh_scores = (
+            lax.dot_general(query, fresh_keys, across, preferred_element_type=F32) * scale
+        )
+        cache_scores = jnp.where(slot_at < len_ref[n], cache_scores, -jnp.inf)
+        fresh_scores = jnp.where(fresh_ok, fresh_scores, -jnp.inf)
+        highest = jnp.maximum(
+            jnp.max(cache_scores, axis=1, keepdims=True),
+            jnp.max(fresh_scores, axis=1, keepdims=True),
+        )
+        cache_exp = jnp.exp(cache_scores - highest)
+        fresh_exp = jnp.exp(fresh_scores - highest)
+        total = jnp.sum(cache_exp, axis=1, keepdims=True) + jnp.sum(
+            fresh_exp, axis=1, keepdims=True
+        )
+        mixed = jnp.dot(
+            (cache_exp / total).astype(BF16), kv_buf[n, 1], preferred_element_type=F32
+        ) + jnp.dot((fresh_exp / total).astype(BF16), fresh_vals, preferred_element_type=F32)
+        padded[pl.ds(pl.multiple_of(n * 8, 8), 8), :] = jnp.concatenate(
+            [mixed[h * 8 : (h + 1) * 8] for h in range(heads)], axis=1
+        )
+        return 0
+
+    lax.fori_loop(0, rr, attend_row, 0, unroll=4)
+
+    attended = padded[...].astype(BF16)
+    row_at = lax.broadcasted_iota(jnp.int32, (rr, 8 * rr), 0)
+    target = row_at * 8
+    for n in range(rr):
+        target = jnp.where(row_at == n, 8 * n + pick_ref[n], target)
+    chosen = lax.broadcasted_iota(jnp.int32, (rr, 8 * rr), 1) == target
+    acc_ref[...] = jnp.dot(
+        jnp.where(chosen, 1.0, 0.0).astype(BF16), attended, preferred_element_type=F32
+    ).astype(BF16)
+
+    def a_copy(j):
+        return remote(acc_ref, acc_in.at[r], a_send.at[j], a_recv.at[j], "rep", tower(j))
+
+    for j in range(1, R):
+        a_copy(j).start()
+    acc_in[r] = acc_ref[...]
+
+    token_at = lax.broadcasted_iota(jnp.int32, (rr * draft_len, 8 * rr), 0)
+    place_at = lax.broadcasted_iota(jnp.int32, (rr * draft_len, 8 * rr), 1)
+    kept = (token_at == place_at - (8 - draft_len) * (place_at // 8)) & (
+        lax.rem(place_at, 8) < draft_len
+    )
+    attn_ref[...] = jnp.dot(
+        jnp.where(kept, 1.0, 0.0).astype(BF16), attended, preferred_element_type=F32
+    ).astype(BF16)
+
 
     for j in range(1, R):
         a_copy(j).wait_recv()
@@ -207,7 +295,7 @@
 
     def rs_copy(i, k):
         return remote(
-            rs_out.at[k], rs_in.at[i, k], rs_send.at[k], rs_recv.at[i, k], "tp", plane(k)
+            rs_out.at[k], rs_in.at[i, k], rs_send.at[k], rs_recv.at[i, k], "tp", flip(t, k, T)
         )
 
     def finish(i):
@@ -223,8 +311,8 @@
     first = acc_in[...].reshape(rows, acc_ref.shape[1])
 
     def project(kk, _):
-        k = lax.rem(kk + 1, T)
-        c = plane(k)
+        k = T - 1 - kk
+        c = flip(t, k, T)
         part[...] = jnp.dot(first, wo_buf[:, cols(c * cw, cw)], preferred_element_type=F32)
 
         @pl.when(r * ratio + c // R == t)
@@ -268,57 +356,87 @@
 
     vb = min(kb, 512)
 
-    def v_copy(kk):
+    def p_copy(n):
         return remote(
-            v_out.at[kk], v_in.at[kk], v_send.at[kk], v_recv.at[kk], "tp", plane(kk + 1)
-        )
-
-    def v_chunk(kk):
-        slot = lax.rem(kk, 2)
-        ws_copy(kk, slot).wait()
+            p_out.at[n], p_in.at[n], p_send.at[n], p_recv.at[n], "tp", chip * 2 + 1 - core
+        )
+
+    def v_copy(n):
+        return remote(
+            v_out.at[n], v_in.at[n], v_send.at[n], v_recv.at[n], "tp", served(n, True)
+        )
+
+    def v_other(n):
+        ws_copy(n, 0).wait()
 
         def block(b, _):
             here = cols(b * vb, vb)
-            v_out[kk, :, here] = jnp.dot(
-                attn_ref[...], ws_buf[slot, :, here], preferred_element_type=F32
+            p_out[n, :, here] = jnp.dot(
+                attn_ref[...], ws_buf[0, :, here], preferred_element_type=F32
             ).astype(BF16)
             return 0
 
         lax.fori_loop(0, kb // vb, block, 0)
-
-        @pl.when(kk < T - 1)
+        p_copy(n).start()
+
+        @pl.when(n < chips - 1)
         def _():
-            v_copy(kk).start()
-
-        @pl.when(kk < T - 2)
+            ws_copy(n + 1, 0).start()
+
+    def v_own(n):
+        ws_copy(n, 1).wait()
+        p_copy(n).wait_recv()
+
+        def block(b, _):
+            here = cols(b * vb, vb)
+            product = jnp.dot(attn_ref[...], ws_buf[1, :, here], preferred_element_type=F32)
+            v_out[n, :, here] = (product + p_in[n, :, here].astype(F32)).astype(BF16)
+            return 0
+
+        lax.fori_loop(0, kb // vb, block, 0)
+
+        @pl.when(n < chips - 1)
         def _():
-            ws_copy(kk + 2, slot).start()
-
-    gaps = 2 * (STEPS - 1)
-    per_gap = -(-T // gaps)
-
-    def v_gap(g):
-        for n in range(per_gap):
-            kk = g * per_gap + n
-
-            @pl.when(kk < T)
+            ws_copy(n + 1, 1).start()
+
+    per_step = -(-chips // (STEPS - 1))
+
+    def each_round(s, top, act):
+        for i in range(per_step):
+            n = s * per_step + i
+
+            @pl.when((n >= 0) & (n < top))
             def _():
-                v_chunk(kk)
-
-    def x_copy(s, j):
+                act(n)
+
+    def x_copy(s, h, j):
         q = tower_back(j)
         target = q * ratio + t // R
-        m = lax.rem(t, R)
+        m = lax.rem(t, R) * halves + h
         return target, remote(
-            z_buf.at[s, q], x_buf.at[s, m], x_send.at[j], x_recv.at[s, m], "tp", target
-        )
-
-    def z_copy(s, j):
-        return remote(z_buf.at[s, r], z_buf.at[s, r], z_send.at[j], z_recv.at[s, j], "rep", tower(j))
-
-    def z_arrival(s, j):
+            z_buf.at[s, h, q], x_buf.at[s, m], x_send.at[h, j], x_recv.at[s, m], "tp", target
+        )
+
+    def z_copy(s, h, j):
+        return remote(
+            z_buf.at[s, h, r],
+            z_buf.at[s, h, r],
+            z_send.at[h, j],
+            z_recv.at[s, h, j],
+            "rep",
+            tower(j),
+        )
+
+    def z_arrival(s, h, j):
         q = tower_back(j)
-        return remote(z_buf.at[s, q], z_buf.at[s, q], z_send.at[j], z_recv.at[s, j], "rep", tower(j))
+        return remote(
+            z_buf.at[s, h, q],
+            z_buf.at[s, h, q],
+            z_send.at[h, j],
+            z_recv.at[s, h, j],
+            "rep",
+            tower(j),
+        )
 
     def sq_copy(s, k):
         return remote(
@@ -327,15 +445,15 @@
 
     def step(s, _):
         mixed = state[...] + emb_f[s]
-        z_buf[s, r] = (mixed * gain_own).astype(BF16)
-        for j in range(1, R):
-            z_copy(s, j).start()
-        for j in range(R):
-            if j == 1:
-                v_gap(2 * s)
-            if j > 0:
-                z_arrival(s, j).wait_recv()
-            target, copy = x_copy(s, j)
+        mixed = (mixed * gain_own).astype(BF16)
+        for h in range(halves):
+            z_buf[s, h, r] = mixed[:, h * hw : (h + 1) * hw]
+        for h in range(halves):
+            for j in range(1, R):
+                z_copy(s, h, j).start()
+
+        def forward(h, j):
+            target, copy = x_copy(s, h, j)
 
             @pl.when(target != t)
             def _():
@@ -343,18 +461,34 @@
 
             @pl.when(target == t)
             def _():
-                x_buf[s, lax.rem(t, R)] = z_buf[s, tower_back(j)]
+                x_buf[s, lax.rem(t, R) * halves + h] = z_buf[s, h, tower_back(j)]
+
+        for h in range(halves):
+            forward(h, 0)
+        each_round(s - 1, chips - 1, lambda n: v_copy(n).start())
+        each_round(s, chips, v_other)
+        for h in range(halves):
+            for j in range(1, R):
+                z_arrival(s, h, j).wait_recv()
+                forward(h, j)
+        each_round(s, chips, v_own)
 
         for m in range(R):
             source = lax.rem(t, ratio) * R + m
 
             @pl.when(source != t)
             def _():
-                remote(
-                    z_buf.at[s, 0], x_buf.at[s, m], x_send.at[0], x_recv.at[s, m], "tp", source
-                ).wait_recv()
-
-        x = jnp.concatenate([x_buf[s, m] for m in range(R)], axis=1)
+                for h in range(halves):
+                    remote(
+                        z_buf.at[s, h, 0],
+                        x_buf.at[s, m * halves + h],
+                        x_send.at[h, 0],
+                        x_recv.at[s, m * halves + h],
+                        "tp",
+                        source,
+                    ).wait_recv()
+
+        x = jnp.concatenate([x_buf[s, m] for m in range(R * halves)], axis=1)
         plain = x.astype(F32) * gain_back
         plain = plain * plain
         lanes = plain[:, :128]
@@ -372,9 +506,9 @@
         sq_in[s, 0] = sq_out[...]
 
         def multiply(kk, _):
-            k = lax.rem(kk + 1, T)
+            k = T - 1 - kk
             product = jnp.dot(
-                x, w_buf[:, cols(plane(k) * cw, cw)], preferred_element_type=F32
+                x, w_buf[:, cols(flip(t, k, T) * cw, cw)], preferred_element_type=F32
             ).astype(BF16)
 
             @pl.when(kk < T - 1)
@@ -389,7 +523,6 @@
             return 0
 
         lax.fori_loop(0, T, multiply, 0)
-        v_gap(2 * s + 1)
         for k in range(1, T):
             sq_copy(s, k).wait_recv()
         squares = sq_in[s, 0]
@@ -407,14 +540,15 @@
         state[...] += update / (1.0 + jnp.exp(-update))
         for k in range(1, T):
             sq_copy(s, k).wait_send()
-        for j in range(1, R):
-            z_copy(s, j).wait_send()
-        for j in range(R):
-            target, copy = x_copy(s, j)
-
-            @pl.when(target != t)
-            def _():
-                copy.wait_send()
+        for h in range(halves):
+            for j in range(1, R):
+                z_copy(s, h, j).wait_send()
+            for j in range(R):
+                target, copy = x_copy(s, h, j)
+
+                @pl.when(target != t)
+                def _():
+                    copy.wait_send()
 
         return 0
 
@@ -431,12 +565,6 @@
         if k > 0:
             f_copy(k).start()
     f_in[t] = f_out[0]
-
-    def v_wait(kk, _):
-        remote(
-            v_out.at[kk], v_in.at[kk], v_send.at[kk], v_recv.at[kk], "tp", plane(kk + 1)
-        ).wait()
-        return 0
 
     for k in range(1, T):
         remote(
@@ -459,14 +587,28 @@
     for j in range(1, R):
         g_copy(j).start()
 
-    lax.fori_loop(0, T - 1, v_wait, 0)
+    def v_wait(n, _):
+        v_copy(n).wait()
+        return 0
+
+    lax.fori_loop(0, chips - 1, v_wait, 0)
+
+    def p_wait(n, _):
+        p_copy(n).wait_send()
+        return 0
+
+    lax.fori_loop(0, chips, p_wait, 0)
 
     def v_sum(b, _):
         here = cols(b * vb, vb)
-        total = v_out[T - 1, :, here].astype(F32)
-        for kk in range(T - 1):
-            total = total + v_in[kk, :, here].astype(F32)
-        ver_ref[:, here] = (resid_ref[:, here].astype(F32) + total).astype(BF16)
+        total = v_out[chips - 1, :, here].astype(F32)
+        for n in range(chips - 1):
+            total = total + v_in[n, :, here].astype(F32)
+        for n in range(rr):
+            ver_ref[n, :, here] = (
+                resid_ref[n, :, here].astype(F32)
+                + total[n * draft_len : (n + 1) * draft_len]
+            ).astype(BF16)
         return 0
 
     lax.fori_loop(0, kb // vb, v_sum, 0)
@@ -511,34 +653,30 @@
     cw = width // (T * R)
     kb = width // T
     nb = width // R
-    group = kdim * T // HEAD_DIM // KV_HEADS
-    kv_start = lax.axis_index("tp") * (kdim // HEAD_DIM) // group * HEAD_DIM
-    own_cache = lax.dynamic_slice_in_dim(kv_cache, kv_start, HEAD_DIM, 3)
-    own_fresh = lax.dynamic_slice_in_dim(kv_new, kv_start, HEAD_DIM, 3)
-    attn = attend(
-        queries, own_cache[:, 0], own_cache[:, 1], own_fresh[:, 0], own_fresh[:, 1], cache_len
-    )
-    picked = (jnp.arange(draft_len, dtype=jnp.int32)[None, :] == accepted[:, None])[:, :, None]
-
-    def pick(array):
-        return jnp.sum(jnp.where(picked, array.astype(F32), 0.0), axis=1).astype(BF16)
-
+    halves = 2 if cw >= 256 else 1
     emb = draft_emb.transpose(1, 0, 2).reshape(steps * own_rows, width)
     emb_rows = -(-steps * own_rows // 16) * 16
     emb = jnp.pad(emb, ((0, emb_rows - steps * own_rows), (0, 0)))
     token_rows = row_count * draft_len
     dma = pltpu.SemaphoreType.DMA
     vmem = pl.BlockSpec(memory_space=pltpu.VMEM)
+    smem = pl.BlockSpec(memory_space=pltpu.SMEM)
     hbm = pl.BlockSpec(memory_space=pl.ANY)
     verified, features = pl.pallas_call(
         functools.partial(fused, T, R, steps),
         out_shape=(
-            jax.ShapeDtypeStruct((token_rows, kb), BF16),
+            jax.ShapeDtypeStruct((row_count, draft_len, kb), BF16),
             jax.ShapeDtypeStruct((own_rows, width), BF16),
         ),
-        in_specs=[vmem] * 5 + [hbm] * 3,
+        in_specs=[smem] * 2 + [vmem] * 4 + [hbm] * 4,
         out_specs=(vmem, vmem),
         scratch_shapes=[
+            pltpu.VMEM((row_count, 2, kv_cache.shape[2], HEAD_DIM), BF16),
+            pltpu.VMEM((8 * row_count, kdim), F32),
+            pltpu.VMEM((token_rows, kdim), BF16),
+            pltpu.VMEM((row_count, kdim), BF16),
+            pltpu.VMEM((row_count, kb), F32),
+            pltpu.VMEM((row_count, kb), BF16),
             pltpu.VMEM((kb, nb), BF16),
             pltpu.VMEM((kdim, nb), BF16),
             pltpu.VMEM((2, kdim, kb), BF16),
@@ -552,13 +690,16 @@
             pltpu.VMEM((steps + 1, T, rows, cw), BF16),
             pltpu.VMEM((8, 128), F32),
             pltpu.VMEM((steps, T, 8, 128), F32),
-            pltpu.VMEM((steps, R, rows, cw), BF16),
-            pltpu.VMEM((steps, R, rows, cw), BF16),
+            pltpu.VMEM((steps, halves, R, rows, cw // halves), BF16),
+            pltpu.VMEM((steps, R * halves, rows, cw // halves), BF16),
             pltpu.VMEM((T, 16, cw), BF16),
             pltpu.VMEM((T, 16, cw), BF16),
             pltpu.VMEM((R, 16, nb // 2), BF16),
-            pltpu.VMEM((T, token_rows, kb), BF16),
-            pltpu.VMEM((T, token_rows, kb), BF16),
+            pltpu.VMEM((T // 2, token_rows, kb), BF16),
+            pltpu.VMEM((T // 2, token_rows, kb), BF16),
+            pltpu.VMEM((T // 2, token_rows, kb), BF16),
+            pltpu.VMEM((T // 2, token_rows, kb), BF16),
+            dma,
             dma,
             dma,
             dma((2,)),
@@ -572,32 +713,36 @@
             dma((steps + 1, T)),
             dma((T,)),
             dma((steps, T)),
-            dma((R,)),
-            dma((steps, R)),
-            dma((R,)),
-            dma((steps, R)),
+            dma((halves, R)),
+            dma((steps, halves, R)),
+            dma((halves, R)),
+            dma((steps, R * halves)),
             dma((T,)),
             dma((T,)),
             dma((R,)),
             dma((R,)),
-            dma((T,)),
-            dma((T,)),
+            dma((T // 2,)),
+            dma((T // 2,)),
+            dma((T // 2,)),
+            dma((T // 2,)),
         ],
         compiler_params=pltpu.CompilerParams(
             collective_id=0, has_side_effects=True, vmem_limit_bytes=56 * 2**20
         ),
         name="verify_and_draft",
     )(
-        attn.reshape(token_rows, kdim),
-        pick(attn),
-        residual.reshape(token_rows, kb),
-        pick(residual),
+        cache_len,
+        accepted,
+        queries,
+        kv_new,
+        residual,
         draft_gain.astype(F32).reshape(1, width),
+        kv_cache,
         emb,
         out_proj,
         draft_proj,
     )
-    return verified.reshape(row_count, draft_len, kb), features
+    return verified, features
 
 
 def solution(mesh):

time: 175 us -> 148 us (0.85)
  Pallas kernels: 154 us -> 134 us
  matrix products: 4.45 us -> 0 us
  other arithmetic: 5.16 us -> 1.38 us
    pallas_call x1, Pallas kernels: 154 us -> 134 us  [local(): pl.pallas_call(functools.partial(fused, T, R, steps), out_shape=(jax.Shap...]
    dot_general x4 -> x0, matrix products: 4.45 us -> none  [the longest x1 1.79 us: attend(): jnp.einsum('rjgd,rpd->rjgp', query_all, cache_keys, preferred_element_typ...]
    reduce_sum x3 -> x0, other arithmetic: 2.2 us -> none  [the longest x1 1.75 us: pick(): jnp.sum(jnp.where(picked, array.astype(F32), 0.0), axis=1).astype(BF16)]
    pallas_call x0 -> x1, local copies, waits for them, and re-layouts: none -> 1.99 us  [local(): pl.pallas_call(functools.partial(fused, T, R, steps), out_shape=(jax.Shap...]
    reshape x2 -> x0, local copies, waits for them, and re-layouts: 1.97 us -> none  [the longest x1 1.11 us: local(): return (verified.reshape(row_count, draft_len, kb), features)]
    unnamed x8 -> x4, local copies, waits for them, and re-layouts: 6.02 us -> 7.01 us
where the time goes in v2:
time: 148 us
  Pallas kernels  134 us (91%)
  local copies, waits for them, and re-layouts  11.6 us (8%)
    pallas_call x1, Pallas kernels, local(): pl.pallas_call(functools.partial(fused, T, R, steps), out_shape=(jax.Shap...  134 us
    unnamed x4, local copies, waits for them, and re-layouts  7.01 us

profile of v2, /device:TPU:0, one launch (start us, length us, event | category | flops | bytes accessed | tf_op | source)
XLA Modules:
  0.0 147.5 jit_solution(4503526891863002915)
XLA Ops:
  0.6 1.4 reshape.15
  2.0 1.7 %copy.12.q_ref = bf16[16,5,1024]{2,1,0:T(8,128)(2,1)} copy(bf16[16,5,1024]{2,0,1:T(8,128)(2,1)} %param.10) | data formatting | bytes 327680 | tf_op args[0]
  3.7 1.6 %copy.13.fresh_ref = bf16[16,2,5,512]{3,2,1,0:T(8,128)(2,1)} copy(bf16[16,2,5,512]{3,1,2,0:T(2,128)(2,1)} %param.12) | data formatting | bytes 327680 | tf_op args[2]
  5.4 2.0 %copy.14.resid_ref = bf16[16,5,2048]{2,1,0:T(8,128)(2,1)} copy(bf16[16,5,2048]{2,0,1:T(8,128)(2,1)} %param.15) | data formatting | bytes 655360 | tf_op args[5]
  7.4 2.6 %pad.4.emb_ref = bf16[48,16384]{1,0:T(8,128)(2,1)} pad(bf16[40,16384]{1,0:T(8,128)(2,1)} %bitcast.4, bf16[]{:T(256)} %constant.2.clone.1), padding=0_8x0_0 | pad | bytes 2883586 | tf_op jit(solution)/shard_map/jit(_pad)/pad | solution.py:659
  9.9 133.9 %verify_and_draft.1 = (bf16[16,5,2048]{2,1,0:T(8,128)(2,1)}, bf16[8,16384]{1,0:T(8,128)(2,1)}) custom-call(s32[16]{0:T(128)} %len_ref.1, s32[16]{0:T(128)} %pick_ref.1, bf16[16,5,1024]{2,1,0:T(8,128)(2,1)} %copy.12.q_ref, bf16[16,2,5,512]{3,2,1,0:T(8,128)(2,1)} %copy.13.fresh_ref, bf16[16,5,2048]{2,1,0:T(8,128)(2,1)} %copy.14.resid_ref, f32[1,16384]{1,0:T(1,128)} %bitcast.5, ...), custom_call_target="tpu_custom_call" | custom-call | tf_op jit(solution)/shard_map/verify_and_draft/pallas_call | solution.py:665
  143.9 2.0 %copy.15 = bf16[16,5,2048]{2,0,1:T(8,128)(2,1)} copy(bf16[16,5,2048]{2,1,0:T(8,128)(2,1)} %get-tuple-element.2) | data formatting | bytes 655360 | tf_op jit(solution)/shard_map/verify_and_draft/pallas_call | solution.py:665
  145.8 1.7 %copy.17 = bf16[8,16384]{1,0:T(8,128)(2,1)} copy(bf16[8,16384]{1,0:T(8,128)(2,1)} %get-tuple-element.7) | data formatting | bytes 524288

commit v3 on v2

--- a/solution.py
+++ b/solution.py
@@ -25,8 +25,8 @@
     fresh_ref,
     resid_ref,
     gain_ref,
+    emb_raw,
     kv_ref,
-    emb_ref,
     oproj_ref,
     dproj_ref,
     ver_ref,
@@ -35,8 +35,9 @@
     padded,
     attn_ref,
     acc_ref,
-    racc_f,
     racc_ref,
+    emb_ref,
+    acc_f,
     w_buf,
     wo_buf,
     ws_buf,
@@ -94,7 +95,9 @@
     kb = width // T
     nb = width // R
     own_rows = rows // T
-    rr, draft_len, kdim = q_ref.shape
+    rr = acc_ref.shape[0]
+    tokens, kdim = q_ref.shape
+    draft_len = tokens // rr
     heads = kdim // HEAD_DIM
     chips = T // 2
     core = lax.rem(t, 2)
@@ -151,14 +154,27 @@
             oproj_ref.at[:, cols(served(n, own) * kb, kb)], ws_buf.at[own], ws_sem.at[own]
         )
 
-    def pick_row(n, _):
-        block = resid_ref[n].astype(F32)
-        chosen = lax.broadcasted_iota(jnp.int32, block.shape, 0) == pick_ref[n]
-        racc_f[pl.ds(n, 1), :] = jnp.sum(jnp.where(chosen, block, 0.0), axis=0, keepdims=True)
+    row_at = lax.broadcasted_iota(jnp.int32, (rr, 128), 0)
+    picked = row_at * 0
+    for n in range(rr):
+        picked = jnp.where(row_at == n, pick_ref[n], picked)
+    picked = picked[:, :1]
+    chosen = jnp.zeros((rr, kb), F32)
+    for i in range(draft_len):
+        chosen = jnp.where(picked == i, resid_ref[i * rr : (i + 1) * rr, :].astype(F32), chosen)
+    racc_ref[...] = chosen.astype(BF16)
+
+    emb_rows = emb_ref.shape[0]
+    emb_blank = jnp.zeros((emb_rows - emb_raw.shape[0], nb // 2), F32)
+
+    def tile_up(b, _):
+        here = cols(b * (nb // 2), nb // 2)
+        emb_ref[:, here] = jnp.concatenate(
+            [emb_raw[:, here].astype(F32), emb_blank], axis=0
+        ).astype(BF16)
         return 0
 
-    lax.fori_loop(0, rr, pick_row, 0)
-    racc_ref[...] = racc_f[...].astype(BF16)
+    lax.fori_loop(0, 2 * R, tile_up, 0)
 
     barrier = pltpu.get_barrier_semaphore()
     for k in range(1, T):
@@ -204,6 +220,14 @@
     ws_copy(0, 0).start()
     ws_copy(0, 1).start()
 
+    place_at = lax.broadcasted_iota(jnp.int32, (8 * rr, tokens), 0)
+    token_at = lax.broadcasted_iota(jnp.int32, (8 * rr, tokens), 1)
+    spread = (token_at == lax.rem(place_at, 8) * rr + place_at // 8) & (
+        lax.rem(place_at, 8) < draft_len
+    )
+    padded[...] = jnp.dot(
+        jnp.where(spread, 1.0, 0.0).astype(BF16), q_ref[...], preferred_element_type=F32
+    )
     kv_copy.wait()
     tall = 8 * heads
     scale = HEAD_DIM ** (-0.5)
@@ -213,19 +237,18 @@
     slot_at = lax.broadcasted_iota(jnp.int32, (tall, slots), 1)
     across = (((1,), (1,)), ((), ()))
     fresh_cols = cols(kv_group * HEAD_DIM, HEAD_DIM)
-    empty = jnp.zeros((8 - draft_len, kdim), F32)
     unused = jnp.zeros((128 - draft_len, HEAD_DIM), F32)
 
     def attend_row(n, _):
-        query = jnp.concatenate([q_ref[n].astype(F32), empty], axis=0)
+        query = padded[pl.ds(pl.multiple_of(n * 8, 8), 8), :]
         query = jnp.concatenate(
             [query[:, h * HEAD_DIM : (h + 1) * HEAD_DIM] for h in range(heads)], axis=0
         ).astype(BF16)
         fresh_keys = jnp.concatenate(
-            [fresh_ref[n, 0, :, fresh_cols].astype(F32), unused], axis=0
+            [fresh_ref[n, :, 0, fresh_cols].astype(F32), unused], axis=0
         ).astype(BF16)
         fresh_vals = jnp.concatenate(
-            [fresh_ref[n, 1, :, fresh_cols].astype(F32), unused], axis=0
+            [fresh_ref[n, :, 1, fresh_cols].astype(F32), unused], axis=0
         ).astype(BF16)
         cache_scores = (
             lax.dot_general(query, kv_buf[n, 0], across, preferred_element_type=F32) * scale
@@ -256,10 +279,7 @@
 
     attended = padded[...].astype(BF16)
     row_at = lax.broadcasted_iota(jnp.int32, (rr, 8 * rr), 0)
-    target = row_at * 8
-    for n in range(rr):
-        target = jnp.where(row_at == n, 8 * n + pick_ref[n], target)
-    chosen = lax.broadcasted_iota(jnp.int32, (rr, 8 * rr), 1) == target
+    chosen = lax.broadcasted_iota(jnp.int32, (rr, 8 * rr), 1) == row_at * 8 + picked
     acc_ref[...] = jnp.dot(
         jnp.where(chosen, 1.0, 0.0).astype(BF16), attended, preferred_element_type=F32
     ).astype(BF16)
@@ -271,9 +291,9 @@
         a_copy(j).start()
     acc_in[r] = acc_ref[...]
 
-    token_at = lax.broadcasted_iota(jnp.int32, (rr * draft_len, 8 * rr), 0)
-    place_at = lax.broadcasted_iota(jnp.int32, (rr * draft_len, 8 * rr), 1)
-    kept = (token_at == place_at - (8 - draft_len) * (place_at // 8)) & (
+    token_at = lax.broadcasted_iota(jnp.int32, (tokens, 8 * rr), 0)
+    place_at = lax.broadcasted_iota(jnp.int32, (tokens, 8 * rr), 1)
+    kept = (token_at == lax.rem(place_at, 8) * rr + place_at // 8) & (
         lax.rem(place_at, 8) < draft_len
     )
     attn_ref[...] = jnp.dot(
@@ -351,8 +371,8 @@
     state[...] = finish(0).astype(BF16).astype(F32)
     w_copy.wait()
 
-    gain_own = gain_ref[:, cols((r * T + t) * cw, cw)]
-    gain_back = 1.0 / gain_ref[:, cols(t * kb, kb)]
+    gain_own = gain_ref[:, cols((r * T + t) * cw, cw)].astype(F32)
+    gain_back = 1.0 / gain_ref[:, cols(t * kb, kb)].astype(F32)
 
     vb = min(kb, 512)
 
@@ -471,14 +491,15 @@
             for j in range(1, R):
                 z_arrival(s, h, j).wait_recv()
                 forward(h, j)
-        each_round(s, chips, v_own)
-
-        for m in range(R):
-            source = lax.rem(t, ratio) * R + m
-
-            @pl.when(source != t)
-            def _():
-                for h in range(halves):
+            if h == 0:
+                each_round(s, chips, v_own)
+
+        def arrive(h):
+            for m in range(R):
+                source = lax.rem(t, ratio) * R + m
+
+                @pl.when(source != t)
+                def _():
                     remote(
                         z_buf.at[s, h, 0],
                         x_buf.at[s, m * halves + h],
@@ -488,12 +509,54 @@
                         source,
                     ).wait_recv()
 
-        x = jnp.concatenate([x_buf[s, m] for m in range(R * halves)], axis=1)
-        plain = x.astype(F32) * gain_back
-        plain = plain * plain
-        lanes = plain[:, :128]
-        for b in range(1, kb // 128):
-            lanes = lanes + plain[:, b * 128 : (b + 1) * 128]
+        def product(h, other):
+            here = cols(flip(chip, other, chips) * 2 * cw, 2 * cw)
+            total = jnp.dot(
+                x_buf[s, h], w_buf[h * hw : (h + 1) * hw, here], preferred_element_type=F32
+            )
+            for m in range(1, R):
+                total = total + jnp.dot(
+                    x_buf[s, m * halves + h],
+                    w_buf[m * cw + h * hw : m * cw + (h + 1) * hw, here],
+                    preferred_element_type=F32,
+                )
+            return total
+
+        for h in range(halves - 1):
+            arrive(h)
+
+            def begin(n, _):
+                other = chips - 1 - n
+                total = product(h, other)
+                acc_f[other] = total if h == 0 else acc_f[other] + total
+                return 0
+
+            lax.fori_loop(0, chips, begin, 0)
+        arrive(halves - 1)
+
+        def complete(n, _):
+            other = chips - 1 - n
+            total = product(halves - 1, other)
+            if halves > 1:
+                total = acc_f[other] + total
+            total = total.astype(BF16)
+            rs_out[2 * other + core] = total[:, :cw]
+            rs_out[2 * other + 1 - core] = total[:, cw:]
+            rs_copy(s + 1, 2 * other + 1).start()
+
+            @pl.when(other > 0)
+            def _():
+                rs_copy(s + 1, 2 * other).start()
+
+            return 0
+
+        lax.fori_loop(0, chips // 2, complete, 0)
+        lanes = jnp.zeros((rows, 128), F32)
+        for m in range(R * halves):
+            plain = x_buf[s, m].astype(F32) * gain_back[:, m * hw : (m + 1) * hw]
+            plain = plain * plain
+            for b in range(hw // 128):
+                lanes = lanes + plain[:, b * 128 : (b + 1) * 128]
         sq_out[:, :rows] = lax.dot_general(
             jnp.ones((8, 128), F32),
             lanes,
@@ -504,25 +567,8 @@
         for k in range(1, T):
             sq_copy(s, k).start()
         sq_in[s, 0] = sq_out[...]
-
-        def multiply(kk, _):
-            k = T - 1 - kk
-            product = jnp.dot(
-                x, w_buf[:, cols(flip(t, k, T) * cw, cw)], preferred_element_type=F32
-            ).astype(BF16)
-
-            @pl.when(kk < T - 1)
-            def _():
-                rs_out[k] = product
-                rs_copy(s + 1, k).start()
-
-            @pl.when(kk == T - 1)
-            def _():
-                rs_in[s + 1, 0] = product
-
-            return 0
-
-        lax.fori_loop(0, T, multiply, 0)
+        lax.fori_loop(chips // 2, chips, complete, 0)
+        rs_in[s + 1, 0] = rs_out[0]
         for k in range(1, T):
             sq_copy(s, k).wait_recv()
         squares = sq_in[s, 0]
@@ -604,11 +650,7 @@
         total = v_out[chips - 1, :, here].astype(F32)
         for n in range(chips - 1):
             total = total + v_in[n, :, here].astype(F32)
-        for n in range(rr):
-            ver_ref[n, :, here] = (
-                resid_ref[n, :, here].astype(F32)
-                + total[n * draft_len : (n + 1) * draft_len]
-            ).astype(BF16)
+        ver_ref[:, here] = (resid_ref[:, here].astype(F32) + total).astype(BF16)
         return 0
 
     lax.fori_loop(0, kb // vb, v_sum, 0)
@@ -654,9 +696,7 @@
     kb = width // T
     nb = width // R
     halves = 2 if cw >= 256 else 1
-    emb = draft_emb.transpose(1, 0, 2).reshape(steps * own_rows, width)
     emb_rows = -(-steps * own_rows // 16) * 16
-    emb = jnp.pad(emb, ((0, emb_rows - steps * own_rows), (0, 0)))
     token_rows = row_count * draft_len
     dma = pltpu.SemaphoreType.DMA
     vmem = pl.BlockSpec(memory_space=pltpu.VMEM)
@@ -665,18 +705,19 @@
     verified, features = pl.pallas_call(
         functools.partial(fused, T, R, steps),
         out_shape=(
-            jax.ShapeDtypeStruct((row_count, draft_len, kb), BF16),
+            jax.ShapeDtypeStruct((token_rows, kb), BF16),
             jax.ShapeDtypeStruct((own_rows, width), BF16),
         ),
-        in_specs=[smem] * 2 + [vmem] * 4 + [hbm] * 4,
+        in_specs=[smem] * 2 + [vmem] * 5 + [hbm] * 3,
         out_specs=(vmem, vmem),
         scratch_shapes=[
             pltpu.VMEM((row_count, 2, kv_cache.shape[2], HEAD_DIM), BF16),
             pltpu.VMEM((8 * row_count, kdim), F32),
             pltpu.VMEM((token_rows, kdim), BF16),
             pltpu.VMEM((row_count, kdim), BF16),
-            pltpu.VMEM((row_count, kb), F32),
             pltpu.VMEM((row_count, kb), BF16),
+            pltpu.VMEM((emb_rows, width), BF16),
+            pltpu.VMEM((T // 2, rows, 2 * cw), F32),
             pltpu.VMEM((kb, nb), BF16),
             pltpu.VMEM((kdim, nb), BF16),
             pltpu.VMEM((2, kdim, kb), BF16),
@@ -733,16 +774,16 @@
     )(
         cache_len,
         accepted,
-        queries,
-        kv_new,
-        residual,
-        draft_gain.astype(F32).reshape(1, width),
+        queries.transpose(1, 0, 2).reshape(token_rows, kdim),
+        kv_new.transpose(0, 2, 1, 3),
+        residual.transpose(1, 0, 2).reshape(token_rows, kb),
+        draft_gain.reshape(1, width),
+        draft_emb.transpose(1, 0, 2).reshape(steps * own_rows, width),
         kv_cache,
-        emb,
         out_proj,
         draft_proj,
     )
-    return verified, features
+    return verified.reshape(draft_len, row_count, kb).transpose(1, 0, 2), features
 
 
 def solution(mesh):

time: 148 us -> 146 us (0.986)
  local copies, waits for them, and re-layouts: 11.6 us -> 4.81 us
  Pallas kernels: 134 us -> 140 us
    pallas_call x1, Pallas kernels: 134 us -> 140 us  [local(): pl.pallas_call(functools.partial(fused, T, R, steps), out_shape=(jax.Shap...]
    unnamed x4 -> x2, local copies, waits for them, and re-layouts: 7.01 us -> 3.39 us
    pad x1 -> x0, local copies, waits for them, and re-layouts: 2.58 us -> none  [local(): emb = jnp.pad(emb, ((0, emb_rows - steps * own_rows), (0, 0)))]
    pallas_call x1 -> x0, local copies, waits for them, and re-layouts: 1.99 us -> none  [local(): pl.pallas_call(functools.partial(fused, T, R, steps), out_shape=(jax.Shap...]
where the time goes in v3:
time: 146 us
  Pallas kernels  140 us (96%)
  local copies, waits for them, and re-layouts  4.81 us (3%)
    pallas_call x1, Pallas kernels, local(): pl.pallas_call(functools.partial(fused, T, R, steps), out_shape=(jax.Shap...  140 us
    unnamed x2, local copies, waits for them, and re-layouts  3.39 us

profile of v3, /device:TPU:0, one launch (start us, length us, event | category | flops | bytes accessed | tf_op | source)
XLA Modules:
  0.0 145.8 jit_solution(6090724937685358766)
XLA Ops:
  0.6 1.4 reshape.21.gain_ref
  2.1 140.3 %verify_and_draft.1 = (bf16[80,2048]{1,0:T(8,128)(2,1)}, bf16[8,16384]{1,0:T(8,128)(2,1)}) custom-call(s32[16]{0:T(128)} %len_ref.1, s32[16]{0:T(128)} %pick_ref.1, bf16[80,1024]{1,0:T(8,128)(2,1)} %bitcast.16, bf16[16,5,2,512]{3,2,1,0:T(2,128)(2,1)} %bitcast.17, bf16[80,2048]{1,0:T(8,128)(2,1)} %bitcast.14, bf16[1,16384]{1,0:T(2,128)(2,1)} %reshape.21.gain_ref, ...), custom_call_target="tpu_custom_call" | custom-call | tf_op jit(solution)/shard_map/verify_and_draft/pallas_call | solution.py:705
  142.4 1.7 %copy.14 = bf16[16,5,2048]{2,0,1:T(8,128)(2,1)} copy(bf16[16,5,2048]{2,0,1:T(8,128)(2,1)} %bitcast.15) | data formatting | bytes 655360
  144.1 1.7 %copy.15 = bf16[8,16384]{1,0:T(8,128)(2,1)} copy(bf16[8,16384]{1,0:T(8,128)(2,1)} %get-tuple-element.9) | data formatting | bytes 524288

commit v4 on v3

--- a/solution.py
+++ b/solution.py
@@ -37,7 +37,6 @@
     acc_ref,
     racc_ref,
     emb_ref,
-    acc_f,
     w_buf,
     wo_buf,
     ws_buf,
@@ -102,7 +101,7 @@
     chips = T // 2
     core = lax.rem(t, 2)
     chip = t // 2
-    halves, hw = x_buf.shape[1] // R, x_buf.shape[3]
+    halves, hw = z_buf.shape[1], z_buf.shape[4]
 
     def plane(k):
         return lax.rem(t + k, T)
@@ -164,18 +163,6 @@
         chosen = jnp.where(picked == i, resid_ref[i * rr : (i + 1) * rr, :].astype(F32), chosen)
     racc_ref[...] = chosen.astype(BF16)
 
-    emb_rows = emb_ref.shape[0]
-    emb_blank = jnp.zeros((emb_rows - emb_raw.shape[0], nb // 2), F32)
-
-    def tile_up(b, _):
-        here = cols(b * (nb // 2), nb // 2)
-        emb_ref[:, here] = jnp.concatenate(
-            [emb_raw[:, here].astype(F32), emb_blank], axis=0
-        ).astype(BF16)
-        return 0
-
-    lax.fori_loop(0, 2 * R, tile_up, 0)
-
     barrier = pltpu.get_barrier_semaphore()
     for k in range(1, T):
         pl.semaphore_signal(barrier, inc=1, device_id={"tp": plane(k)}, device_id_type=MESH)
@@ -200,23 +187,6 @@
     w_copy = pltpu.make_async_copy(dproj_ref, w_buf, w_sem)
     w_copy.start()
 
-    def e_copy(k):
-        return remote(
-            emb_ref.at[:, cols((r * T + plane(k)) * cw, cw)],
-            emb_in.at[k],
-            e_send.at[k],
-            e_recv.at[k],
-            "tp",
-            plane(k),
-        )
-
-    e_own = pltpu.make_async_copy(
-        emb_ref.at[:, cols((r * T + t) * cw, cw)], emb_in.at[0], e_send.at[0]
-    )
-    e_own.start()
-
-    for k in range(1, T):
-        e_copy(k).start()
     ws_copy(0, 0).start()
     ws_copy(0, 1).start()
 
@@ -291,6 +261,35 @@
         a_copy(j).start()
     acc_in[r] = acc_ref[...]
 
+    emb_rows = emb_ref.shape[0]
+    emb_blank = jnp.zeros((emb_rows - emb_raw.shape[0], nb // 2), F32)
+
+    def tile_up(b, _):
+        here = cols(b * (nb // 2), nb // 2)
+        emb_ref[:, here] = jnp.concatenate(
+            [emb_raw[:, here].astype(F32), emb_blank], axis=0
+        ).astype(BF16)
+        return 0
+
+    lax.fori_loop(0, 2 * R, tile_up, 0)
+
+    def e_copy(k):
+        return remote(
+            emb_ref.at[:, cols((r * T + plane(k)) * cw, cw)],
+            emb_in.at[k],
+            e_send.at[k],
+            e_recv.at[k],
+            "tp",
+            plane(k),
+        )
+
+    e_own = pltpu.make_async_copy(
+        emb_ref.at[:, cols((r * T + t) * cw, cw)], emb_in.at[0], e_send.at[0]
+    )
+    e_own.start()
+
+    for k in range(1, T):
+        e_copy(k).start()
     token_at = lax.broadcasted_iota(jnp.int32, (tokens, 8 * rr), 0)
     place_at = lax.broadcasted_iota(jnp.int32, (tokens, 8 * rr), 1)
     kept = (token_at == lax.rem(place_at, 8) * rr + place_at // 8) & (
@@ -315,7 +314,7 @@
 
     def rs_copy(i, k):
         return remote(
-            rs_out.at[k], rs_in.at[i, k], rs_send.at[k], rs_recv.at[i, k], "tp", flip(t, k, T)
+            rs_out.at[k], rs_in.at[i, k], rs_send.at[i, k], rs_recv.at[i, k], "tp", flip(t, k, T)
         )
 
     def finish(i):
@@ -324,9 +323,11 @@
         total = rs_in[i, 0].astype(F32)
         for k in range(1, T):
             total = total + rs_in[i, k].astype(F32)
+        return total
+
+    def drain_sums(i):
         for k in range(1, T):
             rs_copy(i, k).wait_send()
-        return total
 
     first = acc_in[...].reshape(rows, acc_ref.shape[1])
 
@@ -429,19 +430,27 @@
             def _():
                 act(n)
 
+    def x_place(s, m, h):
+        return x_buf.at[s, :, cols(m * cw + h * hw, hw)]
+
     def x_copy(s, h, j):
         q = tower_back(j)
         target = q * ratio + t // R
-        m = lax.rem(t, R) * halves + h
+        m = lax.rem(t, R)
         return target, remote(
-            z_buf.at[s, h, q], x_buf.at[s, m], x_send.at[h, j], x_recv.at[s, m], "tp", target
+            z_buf.at[s, h, q],
+            x_place(s, m, h),
+            x_send.at[s, h, j],
+            x_recv.at[s, m * halves + h],
+            "tp",
+            target,
         )
 
     def z_copy(s, h, j):
         return remote(
             z_buf.at[s, h, r],
             z_buf.at[s, h, r],
-            z_send.at[h, j],
+            z_send.at[s, h, j],
             z_recv.at[s, h, j],
             "rep",
             tower(j),
@@ -452,7 +461,7 @@
         return remote(
             z_buf.at[s, h, q],
             z_buf.at[s, h, q],
-            z_send.at[h, j],
+            z_send.at[s, h, j],
             z_recv.at[s, h, j],
             "rep",
             tower(j),
@@ -460,8 +469,21 @@
 
     def sq_copy(s, k):
         return remote(
-            sq_out, sq_in.at[s, k], sq_send.at[k], sq_recv.at[s, k], "tp", plane(k)
-        )
+            sq_out, sq_in.at[s, k], sq_send.at[s, k], sq_recv.at[s, k], "tp", plane(k)
+        )
+
+    def drain(s):
+        for k in range(1, T):
+            sq_copy(s, k).wait_send()
+        for h in range(halves):
+            for j in range(1, R):
+                z_copy(s, h, j).wait_send()
+            for j in range(R):
+                target, copy = x_copy(s, h, j)
+
+                @pl.when(target != t)
+                def _():
+                    copy.wait_send()
 
     def step(s, _):
         mixed = state[...] + emb_f[s]
@@ -481,67 +503,48 @@
 
             @pl.when(target == t)
             def _():
-                x_buf[s, lax.rem(t, R) * halves + h] = z_buf[s, h, tower_back(j)]
+                x_buf[s, :, cols(lax.rem(t, R) * cw + h * hw, hw)] = z_buf[
+                    s, h, tower_back(j)
+                ]
 
         for h in range(halves):
             forward(h, 0)
         each_round(s - 1, chips - 1, lambda n: v_copy(n).start())
+        drain_sums(s)
+
+        @pl.when(s > 0)
+        def _():
+            drain(s - 1)
+
         each_round(s, chips, v_other)
         for h in range(halves):
             for j in range(1, R):
                 z_arrival(s, h, j).wait_recv()
                 forward(h, j)
-            if h == 0:
-                each_round(s, chips, v_own)
-
-        def arrive(h):
-            for m in range(R):
-                source = lax.rem(t, ratio) * R + m
-
-                @pl.when(source != t)
-                def _():
+        each_round(s, chips, v_own)
+
+        for m in range(R):
+            source = lax.rem(t, ratio) * R + m
+
+            @pl.when(source != t)
+            def _():
+                for h in range(halves):
                     remote(
                         z_buf.at[s, h, 0],
-                        x_buf.at[s, m * halves + h],
-                        x_send.at[h, 0],
+                        x_place(s, m, h),
+                        x_send.at[s, h, 0],
                         x_recv.at[s, m * halves + h],
                         "tp",
                         source,
                     ).wait_recv()
 
-        def product(h, other):
-            here = cols(flip(chip, other, chips) * 2 * cw, 2 * cw)
-            total = jnp.dot(
-                x_buf[s, h], w_buf[h * hw : (h + 1) * hw, here], preferred_element_type=F32
-            )
-            for m in range(1, R):
-                total = total + jnp.dot(
-                    x_buf[s, m * halves + h],
-                    w_buf[m * cw + h * hw : m * cw + (h + 1) * hw, here],
-                    preferred_element_type=F32,
-                )
-            return total
-
-        for h in range(halves - 1):
-            arrive(h)
-
-            def begin(n, _):
-                other = chips - 1 - n
-                total = product(h, other)
-                acc_f[other] = total if h == 0 else acc_f[other] + total
-                return 0
-
-            lax.fori_loop(0, chips, begin, 0)
-        arrive(halves - 1)
-
-        def complete(n, _):
+        def multiply(n, _):
             other = chips - 1 - n
-            total = product(halves - 1, other)
-            if halves > 1:
-                total = acc_f[other] + total
-            total = total.astype(BF16)
-            rs_out[2 * other + core] = total[:, :cw]
-            rs_out[2 * other + 1 - core] = total[:, cw:]
+            start = flip(chip, other, chips) * 2 * cw
+            for b in range(2):
+                rs_out[2 * other + (1 - core if b else core)] = jnp.dot(
+                    x_buf[s], w_buf[:, cols(start + b * cw, cw)], preferred_element_type=F32
+                ).astype(BF16)
             rs_copy(s + 1, 2 * other + 1).start()
 
             @pl.when(other > 0)
@@ -550,13 +553,12 @@
 
             return 0
 
-        lax.fori_loop(0, chips // 2, complete, 0)
+        lax.fori_loop(0, chips // 2, multiply, 0)
         lanes = jnp.zeros((rows, 128), F32)
-        for m in range(R * halves):
-            plain = x_buf[s, m].astype(F32) * gain_back[:, m * hw : (m + 1) * hw]
-            plain = plain * plain
-            for b in range(hw // 128):
-                lanes = lanes + plain[:, b * 128 : (b + 1) * 128]
+        for b in range(kb // 128):
+            here = slice(b * 128, (b + 1) * 128)
+            plain = x_buf[s, :, here].astype(F32) * gain_back[:, here]
+            lanes = lanes + plain * plain
         sq_out[:, :rows] = lax.dot_general(
             jnp.ones((8, 128), F32),
             lanes,
@@ -567,7 +569,7 @@
         for k in range(1, T):
             sq_copy(s, k).start()
         sq_in[s, 0] = sq_out[...]
-        lax.fori_loop(chips // 2, chips, complete, 0)
+        lax.fori_loop(chips // 2, chips, multiply, 0)
         rs_in[s + 1, 0] = rs_out[0]
         for k in range(1, T):
             sq_copy(s, k).wait_recv()
@@ -584,22 +586,12 @@
         inverse = lax.rsqrt(column / width + 1e-05)
         update = finish(s + 1) * inverse
         state[...] += update / (1.0 + jnp.exp(-update))
-        for k in range(1, T):
-            sq_copy(s, k).wait_send()
-        for h in range(halves):
-            for j in range(1, R):
-                z_copy(s, h, j).wait_send()
-            for j in range(R):
-                target, copy = x_copy(s, h, j)
-
-                @pl.when(target != t)
-                def _():
-                    copy.wait_send()
-
         return 0
 
     sq_out[...] = jnp.zeros_like(sq_out)
     lax.fori_loop(0, STEPS, step, 0)
+    drain_sums(STEPS)
+    drain(STEPS - 1)
 
     def f_copy(k):
         return remote(f_out.at[k], f_in.at[t], f_send.at[k], f_recv.at[k], "tp", plane(k))
@@ -717,7 +709,6 @@
             pltpu.VMEM((row_count, kdim), BF16),
             pltpu.VMEM((row_count, kb), BF16),
             pltpu.VMEM((emb_rows, width), BF16),
-            pltpu.VMEM((T // 2, rows, 2 * cw), F32),
             pltpu.VMEM((kb, nb), BF16),
             pltpu.VMEM((kdim, nb), BF16),
             pltpu.VMEM((2, kdim, kb), BF16),
@@ -732,7 +723,7 @@
             pltpu.VMEM((8, 128), F32),
             pltpu.VMEM((steps, T, 8, 128), F32),
             pltpu.VMEM((steps, halves, R, rows, cw // halves), BF16),
-            pltpu.VMEM((steps, R * halves, rows, cw // halves), BF16),
+            pltpu.VMEM((steps, rows, kb), BF16),
             pltpu.VMEM((T, 16, cw), BF16),
             pltpu.VMEM((T, 16, cw), BF16),
             pltpu.VMEM((R, 16, nb // 2), BF16),
@@ -750,13 +741,13 @@
             dma((R,)),
             dma,
             dma((R,)),
-            dma((T,)),
             dma((steps + 1, T)),
-            dma((T,)),
+            dma((steps + 1, T)),
             dma((steps, T)),
-            dma((halves, R)),
+            dma((steps, T)),
             dma((steps, halves, R)),
-            dma((halves, R)),
+            dma((steps, halves, R)),
+            dma((steps, halves, R)),
             dma((steps, R * halves)),
             dma((T,)),
             dma((T,)),

time: 146 us -> 146 us (level)
  no operation moved by 1% of the time
where the time goes in v4:
time: 146 us
  Pallas kernels  141 us (97%)
  local copies, waits for them, and re-layouts  4.81 us (3%)
    pallas_call x1, Pallas kernels, local(): pl.pallas_call(functools.partial(fused, T, R, steps), out_shape=(jax.Shap...  141 us
    unnamed x2, local copies, waits for them, and re-layouts  3.39 us

profile of v4, /device:TPU:0, one launch (start us, length us, event | category | flops | bytes accessed | tf_op | source)
XLA Modules:
  0.0 146.0 jit_solution(13378966638520539475)
XLA Ops:
  0.6 1.4 reshape.21.gain_ref
  2.1 140.6 %verify_and_draft.1 = (bf16[80,2048]{1,0:T(8,128)(2,1)}, bf16[8,16384]{1,0:T(8,128)(2,1)}) custom-call(s32[16]{0:T(128)} %len_ref.1, s32[16]{0:T(128)} %pick_ref.1, bf16[80,1024]{1,0:T(8,128)(2,1)} %bitcast.16, bf16[16,5,2,512]{3,2,1,0:T(2,128)(2,1)} %bitcast.17, bf16[80,2048]{1,0:T(8,128)(2,1)} %bitcast.14, bf16[1,16384]{1,0:T(2,128)(2,1)} %reshape.21.gain_ref, ...), custom_call_target="tpu_custom_call" | custom-call | tf_op jit(solution)/shard_map/verify_and_draft/pallas_call | solution.py:697
  142.6 1.7 %copy.14 = bf16[16,5,2048]{2,0,1:T(8,128)(2,1)} copy(bf16[16,5,2048]{2,0,1:T(8,128)(2,1)} %bitcast.15) | data formatting | bytes 655360
  144.4 1.7 %copy.15 = bf16[8,16384]{1,0:T(8,128)(2,1)} copy(bf16[8,16384]{1,0:T(8,128)(2,1)} %get-tuple-element.9) | data formatting | bytes 524288

commit v5 on v4

--- a/solution.py
+++ b/solution.py
@@ -46,6 +46,8 @@
     racc_in,
     part,
     state,
+    q_out,
+    q_in,
     rs_out,
     rs_in,
     sq_out,
@@ -69,6 +71,8 @@
     a_recv,
     ra_send,
     ra_recv,
+    q_send,
+    q_recv,
     rs_send,
     rs_recv,
     sq_send,
@@ -153,6 +157,47 @@
             oproj_ref.at[:, cols(served(n, own) * kb, kb)], ws_buf.at[own], ws_sem.at[own]
         )
 
+    barrier = pltpu.get_barrier_semaphore()
+    for k in range(1, T):
+        pl.semaphore_signal(barrier, inc=1, device_id={"tp": plane(k)}, device_id_type=MESH)
+    for j in range(1, R):
+        pl.semaphore_signal(barrier, inc=1, device_id={"rep": tower(j)}, device_id_type=MESH)
+    pl.semaphore_wait(barrier, T - 1 + R - 1)
+
+    straight = emb_raw.shape[0] // 16 * 16
+    emb_rows = emb_in.shape[1]
+
+    def e_parts(k):
+        here = cols((r * T + plane(k)) * cw, cw)
+        return (
+            (emb_raw.at[0:straight, here], emb_in.at[k, 0:straight, :]),
+            (emb_ref.at[:, here], emb_in.at[k, straight:emb_rows, :]),
+        )
+
+    def e_copy(k, p):
+        src, dst = e_parts(k)[p]
+        return remote(src, dst, e_send.at[k, p], e_recv.at[k, p], "tp", plane(k))
+
+    e_own = [
+        pltpu.make_async_copy(*e_parts(0)[p], e_send.at[0, p]) for p in range(2)
+    ]
+    e_own[0].start()
+    for k in range(1, T):
+        e_copy(k, 0).start()
+    emb_blank = jnp.zeros((emb_rows - emb_raw.shape[0], nb // 2), F32)
+
+    def tile_up(b, _):
+        here = cols(b * (nb // 2), nb // 2)
+        emb_ref[:, here] = jnp.concatenate(
+            [emb_raw[straight : emb_raw.shape[0], here].astype(F32), emb_blank], axis=0
+        ).astype(BF16)
+        return 0
+
+    lax.fori_loop(0, 2 * R, tile_up, 0)
+    e_own[1].start()
+    for k in range(1, T):
+        e_copy(k, 1).start()
+
     row_at = lax.broadcasted_iota(jnp.int32, (rr, 128), 0)
     picked = row_at * 0
     for n in range(rr):
@@ -162,13 +207,6 @@
     for i in range(draft_len):
         chosen = jnp.where(picked == i, resid_ref[i * rr : (i + 1) * rr, :].astype(F32), chosen)
     racc_ref[...] = chosen.astype(BF16)
-
-    barrier = pltpu.get_barrier_semaphore()
-    for k in range(1, T):
-        pl.semaphore_signal(barrier, inc=1, device_id={"tp": plane(k)}, device_id_type=MESH)
-    for j in range(1, R):
-        pl.semaphore_signal(barrier, inc=1, device_id={"rep": tower(j)}, device_id_type=MESH)
-    pl.semaphore_wait(barrier, T - 1 + R - 1)
 
     home = t // ratio
     ra_offset = lax.rem(home - r + R, R)
@@ -261,35 +299,6 @@
         a_copy(j).start()
     acc_in[r] = acc_ref[...]
 
-    emb_rows = emb_ref.shape[0]
-    emb_blank = jnp.zeros((emb_rows - emb_raw.shape[0], nb // 2), F32)
-
-    def tile_up(b, _):
-        here = cols(b * (nb // 2), nb // 2)
-        emb_ref[:, here] = jnp.concatenate(
-            [emb_raw[:, here].astype(F32), emb_blank], axis=0
-        ).astype(BF16)
-        return 0
-
-    lax.fori_loop(0, 2 * R, tile_up, 0)
-
-    def e_copy(k):
-        return remote(
-            emb_ref.at[:, cols((r * T + plane(k)) * cw, cw)],
-            emb_in.at[k],
-            e_send.at[k],
-            e_recv.at[k],
-            "tp",
-            plane(k),
-        )
-
-    e_own = pltpu.make_async_copy(
-        emb_ref.at[:, cols((r * T + t) * cw, cw)], emb_in.at[0], e_send.at[0]
-    )
-    e_own.start()
-
-    for k in range(1, T):
-        e_copy(k).start()
     token_at = lax.broadcasted_iota(jnp.int32, (tokens, 8 * rr), 0)
     place_at = lax.broadcasted_iota(jnp.int32, (tokens, 8 * rr), 1)
     kept = (token_at == lax.rem(place_at, 8) * rr + place_at // 8) & (
@@ -312,28 +321,74 @@
 
     wo_copy.wait()
 
-    def rs_copy(i, k):
+    def q_copy(i, other):
         return remote(
-            rs_out.at[k], rs_in.at[i, k], rs_send.at[i, k], rs_recv.at[i, k], "tp", flip(t, k, T)
-        )
+            q_out.at[other],
+            q_in.at[i, other],
+            q_send.at[i, other],
+            q_recv.at[i, other],
+            "tp",
+            chip * 2 + 1 - core,
+        )
+
+    def rs_copy(i, other):
+        return remote(
+            rs_out.at[other],
+            rs_in.at[i, other],
+            rs_send.at[i, other],
+            rs_recv.at[i, other],
+            "tp",
+            flip(chip, other, chips) * 2 + core,
+        )
+
+    def sums(i, multiply, middle):
+        def for_partner(other):
+            q_out[other] = multiply(flip(chip, other, chips) * 2 + 1 - core)
+            q_copy(i, other).start()
+
+        def both(n, _):
+            other = chips - 1 - n
+
+            @pl.when(other > 0)
+            def _():
+                for_partner(other - 1)
+
+            total = multiply(flip(chip, other, chips) * 2 + core)
+            q_copy(i, other).wait_recv()
+            total = (total + q_in[i, other]).astype(BF16)
+
+            @pl.when(other > 0)
+            def _():
+                rs_out[other] = total
+                rs_copy(i, other).start()
+
+            @pl.when(other == 0)
+            def _():
+                rs_in[i, 0] = total
+
+            return 0
+
+        for_partner(chips - 1)
+        lax.fori_loop(0, chips // 2, both, 0)
+        middle()
+        lax.fori_loop(chips // 2, chips, both, 0)
 
     def finish(i):
-        for k in range(1, T):
-            rs_copy(i, k).wait_recv()
         total = rs_in[i, 0].astype(F32)
-        for k in range(1, T):
-            total = total + rs_in[i, k].astype(F32)
+        for other in range(chips - 1, 0, -1):
+            rs_copy(i, other).wait_recv()
+            total = total + rs_in[i, other].astype(F32)
         return total
 
     def drain_sums(i):
-        for k in range(1, T):
-            rs_copy(i, k).wait_send()
+        for other in range(chips):
+            q_copy(i, other).wait_send()
+            if other > 0:
+                rs_copy(i, other).wait_send()
 
     first = acc_in[...].reshape(rows, acc_ref.shape[1])
 
-    def project(kk, _):
-        k = T - 1 - kk
-        c = flip(t, k, T)
+    def project(c):
         part[...] = jnp.dot(first, wo_buf[:, cols(c * cw, cw)], preferred_element_type=F32)
 
         @pl.when(r * ratio + c // R == t)
@@ -342,22 +397,15 @@
                 racc_in[:, :, cols(lax.rem(c, R) * cw, cw)].reshape(rows, cw).astype(F32)
             )
 
-        @pl.when(kk < T - 1)
-        def _():
-            rs_out[k] = part[...].astype(BF16)
-            rs_copy(0, k).start()
-
-        @pl.when(kk == T - 1)
-        def _():
-            rs_in[0, 0] = part[...].astype(BF16)
-
-        return 0
-
-    lax.fori_loop(0, T, project, 0)
-
-    e_own.wait()
+        return part[...]
+
+    sums(0, project, lambda: None)
+
+    for copy in e_own:
+        copy.wait()
     for k in range(1, T):
-        e_copy(k).wait_recv()
+        for p in range(2):
+            e_copy(k, p).wait_recv()
 
     def place(k, _):
         source = lax.rem(t - k + T, T)
@@ -538,39 +586,30 @@
                         source,
                     ).wait_recv()
 
-        def multiply(n, _):
-            other = chips - 1 - n
-            start = flip(chip, other, chips) * 2 * cw
-            for b in range(2):
-                rs_out[2 * other + (1 - core if b else core)] = jnp.dot(
-                    x_buf[s], w_buf[:, cols(start + b * cw, cw)], preferred_element_type=F32
-                ).astype(BF16)
-            rs_copy(s + 1, 2 * other + 1).start()
-
-            @pl.when(other > 0)
-            def _():
-                rs_copy(s + 1, 2 * other).start()
-
-            return 0
-
-        lax.fori_loop(0, chips // 2, multiply, 0)
-        lanes = jnp.zeros((rows, 128), F32)
-        for b in range(kb // 128):
-            here = slice(b * 128, (b + 1) * 128)
-            plain = x_buf[s, :, here].astype(F32) * gain_back[:, here]
-            lanes = lanes + plain * plain
-        sq_out[:, :rows] = lax.dot_general(
-            jnp.ones((8, 128), F32),
-            lanes,
-            (((1,), (1,)), ((), ())),
-            precision=EXACT,
-            preferred_element_type=F32,
-        )
-        for k in range(1, T):
-            sq_copy(s, k).start()
-        sq_in[s, 0] = sq_out[...]
-        lax.fori_loop(chips // 2, chips, multiply, 0)
-        rs_in[s + 1, 0] = rs_out[0]
+        def squares_out():
+            lanes = jnp.zeros((rows, 128), F32)
+            for b in range(kb // 128):
+                here = slice(b * 128, (b + 1) * 128)
+                plain = x_buf[s, :, here].astype(F32) * gain_back[:, here]
+                lanes = lanes + plain * plain
+            sq_out[:, :rows] = lax.dot_general(
+                jnp.ones((8, 128), F32),
+                lanes,
+                (((1,), (1,)), ((), ())),
+                precision=EXACT,
+                preferred_element_type=F32,
+            )
+            for k in range(1, T):
+                sq_copy(s, k).start()
+            sq_in[s, 0] = sq_out[...]
+
+        sums(
+            s + 1,
+            lambda c: jnp.dot(
+                x_buf[s], w_buf[:, cols(c * cw, cw)], preferred_element_type=F32
+            ),
+            squares_out,
+        )
         for k in range(1, T):
             sq_copy(s, k).wait_recv()
         squares = sq_in[s, 0]
@@ -663,7 +702,8 @@
         ra_copy().wait_send()
 
     for k in range(1, T):
-        e_copy(k).wait_send()
+        for p in range(2):
+            e_copy(k, p).wait_send()
 
 
 def local(
@@ -708,7 +748,7 @@
             pltpu.VMEM((token_rows, kdim), BF16),
             pltpu.VMEM((row_count, kdim), BF16),
             pltpu.VMEM((row_count, kb), BF16),
-            pltpu.VMEM((emb_rows, width), BF16),
+            pltpu.VMEM((16, width), BF16),
             pltpu.VMEM((kb, nb), BF16),
             pltpu.VMEM((kdim, nb), BF16),
             pltpu.VMEM((2, kdim, kb), BF16),
@@ -718,8 +758,10 @@
             pltpu.VMEM((R, row_count, kb), BF16),
             pltpu.VMEM((rows, cw), F32),
             pltpu.VMEM((rows, cw), F32),
-            pltpu.VMEM((T, rows, cw), BF16),
-            pltpu.VMEM((steps + 1, T, rows, cw), BF16),
+            pltpu.VMEM((T // 2, rows, cw), F32),
+            pltpu.VMEM((steps + 1, T // 2, rows, cw), F32),
+            pltpu.VMEM((T // 2, rows, cw), BF16),
+            pltpu.VMEM((steps + 1, T // 2, rows, cw), BF16),
             pltpu.VMEM((8, 128), F32),
             pltpu.VMEM((steps, T, 8, 128), F32),
             pltpu.VMEM((steps, halves, R, rows, cw // halves), BF16),
@@ -735,14 +777,16 @@
             dma,
             dma,
             dma((2,)),
-            dma((T,)),
-            dma((T,)),
+            dma((T, 2)),
+            dma((T, 2)),
             dma((R,)),
             dma((R,)),
             dma,
             dma((R,)),
-            dma((steps + 1, T)),
-            dma((steps + 1, T)),
+            dma((steps + 1, T // 2)),
+            dma((steps + 1, T // 2)),
+            dma((steps + 1, T // 2)),
+            dma((steps + 1, T // 2)),
             dma((steps, T)),
             dma((steps, T)),
             dma((steps, halves, R)),

time: 146 us -> 143 us (0.979)
  Pallas kernels: 141 us -> 137 us
    pallas_call x1, Pallas kernels: 141 us -> 137 us  [local(): pl.pallas_call(functools.partial(fused, T, R, steps), out_shape=(jax.Shap...]
where the time goes in v5:
time: 143 us
  Pallas kernels  137 us (96%)
  local copies, waits for them, and re-layouts  4.81 us (3%)
    pallas_call x1, Pallas kernels, local(): pl.pallas_call(functools.partial(fused, T, R, steps), out_shape=(jax.Shap...  137 us
    unnamed x2, local copies, waits for them, and re-layouts  3.39 us

profile of v5, /device:TPU:0, one launch (start us, length us, event | category | flops | bytes accessed | tf_op | source)
XLA Modules:
  0.0 142.6 jit_solution(7467493255952791514)
XLA Ops:
  0.6 1.4 reshape.21.gain_ref
  2.1 137.1 %verify_and_draft.1 = (bf16[80,2048]{1,0:T(8,128)(2,1)}, bf16[8,16384]{1,0:T(8,128)(2,1)}) custom-call(s32[16]{0:T(128)} %len_ref.1, s32[16]{0:T(128)} %pick_ref.1, bf16[80,1024]{1,0:T(8,128)(2,1)} %bitcast.16, bf16[16,5,2,512]{3,2,1,0:T(2,128)(2,1)} %bitcast.17, bf16[80,2048]{1,0:T(8,128)(2,1)} %bitcast.14, bf16[1,16384]{1,0:T(2,128)(2,1)} %reshape.21.gain_ref, ...), custom_call_target="tpu_custom_call" | custom-call | tf_op jit(solution)/shard_map/verify_and_draft/pallas_call | solution.py:737
  139.2 1.7 %copy.14 = bf16[16,5,2048]{2,0,1:T(8,128)(2,1)} copy(bf16[16,5,2048]{2,0,1:T(8,128)(2,1)} %bitcast.15) | data formatting | bytes 655360
  140.9 1.7 %copy.15 = bf16[8,16384]{1,0:T(8,128)(2,1)} copy(bf16[8,16384]{1,0:T(8,128)(2,1)} %get-tuple-element.9) | data formatting | bytes 524288

commit v6 on v5

--- a/solution.py
+++ b/solution.py
@@ -33,6 +33,7 @@
     out_ref,
     kv_buf,
     padded,
+    mixed_ref,
     attn_ref,
     acc_ref,
     racc_ref,
@@ -247,45 +248,58 @@
     fresh_cols = cols(kv_group * HEAD_DIM, HEAD_DIM)
     unused = jnp.zeros((128 - draft_len, HEAD_DIM), F32)
 
-    def attend_row(n, _):
+    def stack(n):
         query = padded[pl.ds(pl.multiple_of(n * 8, 8), 8), :]
-        query = jnp.concatenate(
+        return jnp.concatenate(
             [query[:, h * HEAD_DIM : (h + 1) * HEAD_DIM] for h in range(heads)], axis=0
         ).astype(BF16)
-        fresh_keys = jnp.concatenate(
-            [fresh_ref[n, :, 0, fresh_cols].astype(F32), unused], axis=0
+
+    def fresh(n, which):
+        return jnp.concatenate(
+            [fresh_ref[n, :, which, fresh_cols].astype(F32), unused], axis=0
         ).astype(BF16)
-        fresh_vals = jnp.concatenate(
-            [fresh_ref[n, :, 1, fresh_cols].astype(F32), unused], axis=0
-        ).astype(BF16)
-        cache_scores = (
-            lax.dot_general(query, kv_buf[n, 0], across, preferred_element_type=F32) * scale
-        )
-        fresh_scores = (
-            lax.dot_general(query, fresh_keys, across, preferred_element_type=F32) * scale
-        )
-        cache_scores = jnp.where(slot_at < len_ref[n], cache_scores, -jnp.inf)
-        fresh_scores = jnp.where(fresh_ok, fresh_scores, -jnp.inf)
-        highest = jnp.maximum(
-            jnp.max(cache_scores, axis=1, keepdims=True),
-            jnp.max(fresh_scores, axis=1, keepdims=True),
-        )
-        cache_exp = jnp.exp(cache_scores - highest)
-        fresh_exp = jnp.exp(fresh_scores - highest)
-        total = jnp.sum(cache_exp, axis=1, keepdims=True) + jnp.sum(
-            fresh_exp, axis=1, keepdims=True
-        )
-        mixed = jnp.dot(
-            (cache_exp / total).astype(BF16), kv_buf[n, 1], preferred_element_type=F32
-        ) + jnp.dot((fresh_exp / total).astype(BF16), fresh_vals, preferred_element_type=F32)
-        padded[pl.ds(pl.multiple_of(n * 8, 8), 8), :] = jnp.concatenate(
-            [mixed[h * 8 : (h + 1) * 8] for h in range(heads)], axis=1
+
+    def scores(query, keys):
+        return lax.dot_general(query, keys, across, preferred_element_type=F32) * scale
+
+    def attend_rows(group, _):
+        members = [group * 4 + i for i in range(4)]
+        queries = [stack(n) for n in members]
+        cache_scores = [scores(q, kv_buf[n, 0]) for q, n in zip(queries, members)]
+        fresh_scores = [scores(q, fresh(n, 0)) for q, n in zip(queries, members)]
+        cache_scores = [
+            jnp.where(slot_at < len_ref[n], x, -jnp.inf) for x, n in zip(cache_scores, members)
+        ]
+        fresh_scores = [jnp.where(fresh_ok, x, -jnp.inf) for x in fresh_scores]
+        highest = [
+            jnp.maximum(jnp.max(a, axis=1, keepdims=True), jnp.max(b, axis=1, keepdims=True))
+            for a, b in zip(cache_scores, fresh_scores)
+        ]
+        cache_exp = [jnp.exp(a - m) for a, m in zip(cache_scores, highest)]
+        fresh_exp = [jnp.exp(b - m) for b, m in zip(fresh_scores, highest)]
+        total = [
+            jnp.sum(a, axis=1, keepdims=True) + jnp.sum(b, axis=1, keepdims=True)
+            for a, b in zip(cache_exp, fresh_exp)
+        ]
+        cache_weights = [(a / m).astype(BF16) for a, m in zip(cache_exp, total)]
+        fresh_weights = [(b / m).astype(BF16) for b, m in zip(fresh_exp, total)]
+        mixed = [
+            jnp.dot(a, kv_buf[n, 1], preferred_element_type=F32)
+            + jnp.dot(b, fresh(n, 1), preferred_element_type=F32)
+            for a, b, n in zip(cache_weights, fresh_weights, members)
+        ]
+        mixed_ref[pl.ds(pl.multiple_of(group * 32, 32), 32), :] = jnp.concatenate(
+            [
+                jnp.concatenate([m[h * 8 : (h + 1) * 8] for h in range(heads)], axis=1)
+                for m in mixed
+            ],
+            axis=0,
         )
         return 0
 
-    lax.fori_loop(0, rr, attend_row, 0, unroll=4)
-
-    attended = padded[...].astype(BF16)
+    lax.fori_loop(0, rr // 4, attend_rows, 0)
+
+    attended = mixed_ref[...].astype(BF16)
     row_at = lax.broadcasted_iota(jnp.int32, (rr, 8 * rr), 0)
     chosen = lax.broadcasted_iota(jnp.int32, (rr, 8 * rr), 1) == row_at * 8 + picked
     acc_ref[...] = jnp.dot(
@@ -744,6 +758,7 @@
         out_specs=(vmem, vmem),
         scratch_shapes=[
             pltpu.VMEM((row_count, 2, kv_cache.shape[2], HEAD_DIM), BF16),
+            pltpu.VMEM((8 * row_count, kdim), F32),
             pltpu.VMEM((8 * row_count, kdim), F32),
             pltpu.VMEM((token_rows, kdim), BF16),
             pltpu.VMEM((row_count, kdim), BF16),

time: 143 us -> 138 us (0.965)
  Pallas kernels: 137 us -> 132 us
    pallas_call x1, Pallas kernels: 137 us -> 132 us  [local(): pl.pallas_call(functools.partial(fused, T, R, steps), out_shape=(jax.Shap...]
where the time goes in v6:
time: 138 us
  Pallas kernels  132 us (96%)
  local copies, waits for them, and re-layouts  4.81 us (3%)
    pallas_call x1, Pallas kernels, local(): pl.pallas_call(functools.partial(fused, T, R, steps), out_shape=(jax.Shap...  132 us
    unnamed x2, local copies, waits for them, and re-layouts  3.39 us

profile of v6, /device:TPU:0, one launch (start us, length us, event | category | flops | bytes accessed | tf_op | source)
XLA Modules:
  0.0 137.9 jit_solution(6554895091648236114)
XLA Ops:
  0.6 1.4 %reshape.21.gain_ref = bf16[1,16384]{1,0:T(2,128)(2,1)} reshape(bf16[16384]{0:T(1024)(128)(2,1)} %param.18) | data formatting | bytes 65536 | tf_op jit(solution)/shard_map/reshape | solution.py:830
  2.1 132.4 %verify_and_draft.1 = (bf16[80,2048]{1,0:T(8,128)(2,1)}, bf16[8,16384]{1,0:T(8,128)(2,1)}) custom-call(s32[16]{0:T(128)} %len_ref.1, s32[16]{0:T(128)} %pick_ref.1, bf16[80,1024]{1,0:T(8,128)(2,1)} %bitcast.16, bf16[16,5,2,512]{3,2,1,0:T(2,128)(2,1)} %bitcast.17, bf16[80,2048]{1,0:T(8,128)(2,1)} %bitcast.14, bf16[1,16384]{1,0:T(2,128)(2,1)} %reshape.21.gain_ref, ...), custom_call_target="tpu_custom_call" | custom-call | tf_op jit(solution)/shard_map/verify_and_draft/pallas_call | solution.py:751
  134.5 1.7 %copy.14 = bf16[16,5,2048]{2,0,1:T(8,128)(2,1)} copy(bf16[16,5,2048]{2,0,1:T(8,128)(2,1)} %bitcast.15) | data formatting | bytes 655360
  136.2 1.7 %copy.15 = bf16[8,16384]{1,0:T(8,128)(2,1)} copy(bf16[8,16384]{1,0:T(8,128)(2,1)} %get-tuple-element.9) | data formatting | bytes 524288
